TPU v7x, 256 devices: a whole 4x4x8 slice. The times are simulated.
256 devices in a mesh: dom: 64 (over z, x, core), feat: 4 (over y).
Axes of the slice: x: 4, y: 4, z: 8, core: 2. Of those that a mesh axis runs over, the one named last changes fastest.
Arguments:
- initial: bfloat16 [131072, 256], P('dom', 'feat'), may hold values from -6 to 6
- history: bfloat16 [2, 131072, 256], P(None, 'dom', 'feat'), may hold values from -6 to 6
- adjacency: bfloat16 [131072, 2560], P('dom'), may hold values from 0 to 3, as said below
- tile_mask: int32 [1024, 20], P('dom'), may hold values from 0 to 1
- send_lists: int32 [64, 64, 8], P('dom'), may hold values from 0 to 2047
- weights: bfloat16 [3, 256, 256], P(None, 'feat'), may hold values from -0.375 to 0.375
Outputs:
- embeddings: bfloat16 [131072, 256], P('dom', 'feat')
Inputs may be any that keep to these rules, and one draw needn't show every extreme that they name: adjacency entries are nonnegative.
All inputs are finite; a program needn't handle non-finite values.
Results may differ from a plain program's by a relative error of at most 0.0059.
Values may be sent and summed in bfloat16 or wider, within the bound.
No kernel may reach another device: no remote copies, remote signals or barrier semaphores. Data moves between devices by JAX's collectives and lax.ppermute only.
A program may use at most 64 MiB of HBM per device.

v0:
```python
import jax
import jax.numpy as jnp
from jax import lax
from jax.sharding import PartitionSpec as P


def local(initial, history, adjacency, tile_mask, send_lists, weights):
    tile = 128
    width = initial.shape[1]
    expand = jnp.repeat(jnp.repeat(tile_mask, tile, axis=0), tile, axis=1).astype(jnp.float32)
    masked = adjacency.astype(jnp.float32) * expand
    propagate = (masked / (1.0 + jnp.sum(masked, axis=1, keepdims=True))).astype(jnp.bfloat16)
    targets = send_lists[0]
    peers = targets.shape[0]
    depths = weights.shape[0]
    sources = [initial] + [history[k] for k in range(depths - 1)]
    current = initial
    init_float = initial.astype(jnp.float32)
    for depth in range(depths):
        outgoing = sources[depth][targets]
        arrived = lax.all_to_all(outgoing, "dom", split_axis=0, concat_axis=0, tiled=True)
        border = arrived.reshape(peers * targets.shape[1], width)
        joined = jnp.concatenate([current, border], axis=0)
        aggregate = jnp.dot(propagate, joined, preferred_element_type=jnp.float32)
        support = 0.9 * aggregate + 0.1 * init_float
        support_low = support.astype(jnp.bfloat16)
        beta = jnp.log(0.5 / (depth + 1) + 1.0).astype(jnp.float32)
        partial_sum = jnp.dot(support_low, weights[depth], preferred_element_type=jnp.float32)
        product = lax.psum_scatter(
            partial_sum.astype(jnp.bfloat16), "feat", scatter_dimension=1, tiled=True
        ).astype(jnp.float32)
        current = jax.nn.relu((1.0 - beta) * support + beta * product).astype(jnp.bfloat16)
    return current


def solution(mesh):
    placed = (
        P("dom", "feat"),
        P(None, "dom", "feat"),
        P("dom", None),
        P("dom", None),
        P("dom", None, None),
        P(None, "feat", None),
    )
    return jax.shard_map(
        local, mesh=mesh, in_specs=placed, out_specs=P("dom", "feat"), check_vma=False
    )
```

profile of v0, /device:TPU:1, one launch (start us, length us, event | category | flops | bytes accessed | tf_op | source)
XLA Modules:
  0.0 163.2 jit_solution(12577716980893934959)
XLA Ops:
  6.5 0.7 compare_select_fusion
  7.4 1.2 copy.16
  8.6 1.3 gather_fusion
  10.0 0.8 reshape.79
  10.8 13.0 %all-to-all-start = ((bf16[64,2,256]{2,1,0:T(2,128)(2,1)}), bf16[64,2,256]{2,1,0:T(2,128)(2,1)S(1)}, u32[]{:S(2)}, u32[]{:S(2)}) async-start(bf16[64,2,256]{2,1,0:T(2,128)(2,1)} %reshape.79), calls=%async_computation | async-start | bytes 131072 | tf_op jit(solution)/shard_map/all_to_all | solution.py:21
  23.8 0.7 convert_element_type.57
  24.8 14.5 %copy.13 = bf16[2048,2560]{0,1:T(8,128)(2,1)} copy(bf16[2048,2560]{1,0:T(8,128)(2,1)} %param.8) | data formatting | bytes 20971520 | tf_op args[2]
  39.3 6.3 %fusion = f32[2048]{0:T(1024)S(1)} fusion(bf16[2048,2560]{0,1:T(8,128)(2,1)} %copy.13, f32[2048,20]{0,1:T(8,128)S(1)} %bitcast.38), kind=kLoop, calls=%fused_computation.5 | loop fusion | flops 15726592 | bytes 10657792 | tf_op jit(solution)/shard_map/reduce_sum | solution.py:12
  45.6 0.7 copy-done
  46.3 6.0 %divide_convert_fusion = bf16[2048,2560]{0,1:T(8,128)(2,1)} fusion(bf16[2048,2560]{0,1:T(8,128)(2,1)S(1)} %copy-done, f32[2048]{0:T(1024)S(1)} %broadcast_add_fusion, f32[2048,20]{0,1:T(8,128)S(1)} %bitcast.39), kind=kLoop, calls=%fused_computation.4 | loop fusion | flops 20971520 | bytes 21143552 | tf_op jit(solution)/shard_map/convert_element_type | solution.py:12
  52.3 0.1 reshape.80
  52.6 6.0 %fusion.3 = f32[2048,64]{0,1:T(8,128)S(1)} fusion(bf16[2048,2560]{0,1:T(8,128)(2,1)} %divide_convert_fusion, bf16[2048,64]{0,1:T(8,128)(2,1)S(1)} %copy-done.1, bf16[512,64]{0,1:T(8,128)(2,1)S(1)} %copy.17), kind=kOutput, calls=%fused_computation.14 | convolution fusion | flops 672268288 | bytes 11337728 | tf_op jit(solution)/shard_map/dot_general | solution.py:24
  58.6 1.4 convolution_convert_fusion.2
  60.1 0.3 copy.22
  60.4 1.3 gather_fusion.1
  61.8 0.2 reshape.77
  61.9 20.2 %all_to_all.15 = bf16[64,2,256]{2,1,0:T(2,128)(2,1)S(1)} all-to-all(bf16[64,2,256]{2,1,0:T(2,128)(2,1)S(1)} %reshape.77), channel_id=1, replica_groups=mesh['dom'=64,'feat'=4] {'dom'}, dimensions={0} | all-to-all | bytes 131072 | tf_op jit(solution)/shard_map/all_to_all | solution.py:21
  82.1 0.1 reshape.78
  82.4 3.7 %reduce-scatter.4.cloned.1.call-done = bf16[2048,64]{0,1:T(8,128)(2,1)} async-done(((bf16[2048,256]{0,1:T(8,128)(2,1)}), bf16[2048,64]{0,1:T(8,128)(2,1)}) %reduce-scatter.4.cloned.1.call-update) | async-done | bytes 262160 | tf_op jit(solution)/shard_map/reduce_scatter | solution.py:29
  86.0 1.0 maximum_convert_fusion.2
  87.1 5.9 %fusion.2 = f32[2048,64]{0,1:T(8,128)S(1)} fusion(bf16[2048,2560]{0,1:T(8,128)(2,1)} %divide_convert_fusion, bf16[2048,64]{0,1:T(8,128)(2,1)S(1)} %copy-done.1, bf16[512,64]{0,1:T(8,128)(2,1)S(1)} %copy.19, bf16[2048,64]{0,1:T(8,128)(2,1)S(1)} %maximum_convert_fusion.2), kind=kOutput, calls=%fused_computation.12 | convolution fusion | flops 672268288 | bytes 11599872 | tf_op jit(solution)/shard_map/dot_general | solution.py:24
  93.0 1.4 convolution_convert_fusion.1
  94.5 0.3 copy.23
  94.8 1.3 gather_fusion.2
  96.2 0.2 reshape.75
  96.3 22.1 %all_to_all.16 = bf16[64,2,256]{2,1,0:T(2,128)(2,1)S(1)} all-to-all(bf16[64,2,256]{2,1,0:T(2,128)(2,1)S(1)} %reshape.75), channel_id=1, replica_groups=mesh['dom'=64,'feat'=4] {'dom'}, dimensions={0} | all-to-all | bytes 131072 | tf_op jit(solution)/shard_map/all_to_all | solution.py:21
  118.7 1.1 reduce-scatter.6.cloned.1.call-done
  119.8 1.0 maximum_convert_fusion.1
  120.8 5.9 %fusion.1 = f32[2048,64]{0,1:T(8,128)S(1)} fusion(bf16[2048,2560]{0,1:T(8,128)(2,1)} %divide_convert_fusion, bf16[2048,64]{0,1:T(8,128)(2,1)S(1)} %copy-done.1, bf16[512,64]{0,1:T(8,128)(2,1)S(1)} %copy.21, bf16[2048,64]{0,1:T(8,128)(2,1)S(1)} %maximum_convert_fusion.1), kind=kOutput, calls=%fused_computation.10 | convolution fusion | flops 672268288 | bytes 11599872 | tf_op jit(solution)/shard_map/dot_general | solution.py:24
  126.8 1.4 convolution_convert_fusion
  128.2 26.7 %reduce-scatter.8.cloned.1.call-done = bf16[2048,64]{0,1:T(8,128)(2,1)} async-done(((bf16[2048,256]{0,1:T(8,128)(2,1)}), bf16[2048,64]{0,1:T(8,128)(2,1)}) %reduce-scatter.8.cloned.1.call-update) | async-done | bytes 262160 | tf_op jit(solution)/shard_map/reduce_scatter | solution.py:29
  154.9 1.7 %maximum_convert_fusion = bf16[2048,64]{0,1:T(8,128)(2,1)} fusion(bf16[2048,64]{0,1:T(8,128)(2,1)} %reduce-scatter.8.cloned.1.call-done, f32[2048,64]{0,1:T(8,128)S(1)} %fusion.1), kind=kLoop, calls=%fused_computation.15 | loop fusion | flops 786432 | bytes 1048576 | tf_op jit(solution)/shard_map/convert_element_type | solution.py:32
  (27 shorter events, 1.1 us)
Async XLA Ops:
  10.8 41.5 %all-to-all-start = ((bf16[64,2,256]{2,1,0:T(2,128)(2,1)}), bf16[64,2,256]{2,1,0:T(2,128)(2,1)S(1)}, u32[]{:S(2)}, u32[]{:S(2)}) async-start(bf16[64,2,256]{2,1,0:T(2,128)(2,1)} %reshape.79), calls=%async_computation | async-start | bytes 131072 | tf_op jit(solution)/shard_map/all_to_all | solution.py:21
  23.8 62.3 %reduce-scatter.4.cloned.1.call-start = ((), (), s32[]{:S(2)}) async-start(), calls=%async_computation.6 | async-start | bytes 1310720 | tf_op jit(solution)/shard_map/reduce_scatter | solution.py:29
  39.3 7.0 %copy-start = (bf16[2048,2560]{0,1:T(8,128)(2,1)S(1)}, bf16[2048,2560]{0,1:T(8,128)(2,1)}, u32[]{:S(2)}) copy-start(bf16[2048,2560]{0,1:T(8,128)(2,1)} %copy.13) | copy-start | bytes 31457284
  46.3 6.2 %copy-start.1 = (bf16[2048,64]{0,1:T(8,128)(2,1)S(1)}, bf16[2048,64]{0,1:T(8,128)(2,1)}, u32[]{:S(2)}) copy-start(bf16[2048,64]{0,1:T(8,128)(2,1)} %param.6) | copy-start | bytes 786436
  52.3 6.3 %copy-start.3 = (bf16[3,64,256]{2,1,0:T(8,128)(2,1)S(1)}, bf16[3,64,256]{2,1,0:T(8,128)(2,1)}, u32[]{:S(2)}) copy-start(bf16[3,64,256]{2,1,0:T(8,128)(2,1)} %param.11) | copy-start | bytes 294916
  52.6 7.5 %copy-start.2 = (bf16[2,2048,64]{1,2,0:T(8,128)(2,1)S(1)}, bf16[2,2048,64]{1,2,0:T(8,128)(2,1)}, u32[]{:S(2)}) copy-start(bf16[2,2048,64]{1,2,0:T(8,128)(2,1)} %param.7) | copy-start | bytes 1572868
  60.0 59.8 %reduce-scatter.6.cloned.1.call-start = ((), (), s32[]{:S(2)}) async-start(), calls=%async_computation.7 | async-start | bytes 1310720 | tf_op jit(solution)/shard_map/reduce_scatter | solution.py:29
  94.5 60.4 %reduce-scatter.8.cloned.1.call-start = ((), (), s32[]{:S(2)}) async-start(), calls=%async_computation.8 | async-start | bytes 1310720 | tf_op jit(solution)/shard_map/reduce_scatter | solution.py:29
Sparse Core Ops, SparseCore 0:
  60.2 25.8 reduce-scatter.3
  94.6 25.1 reduce-scatter.5
  128.3 26.5 reduce-scatter.7
where the time goes:
time: 165 us; the launch traced here: 163 us
  blocking collectives  42.3 us (26%)
  waiting for transfers between devices  31.6 us (19%)
  local copies, waits for them, and re-layouts  23.3 us (14%)
  matrix products  22.1 us (13%)
  other arithmetic  17.5 us (11%)
  between operations  13.3 us (8%)
  starting transfers between devices  13.1 us (8%)
    all_to_all x2, blocking collectives, local(): lax.all_to_all(outgoing, 'dom', split_axis=0, concat_axis=0, tiled=True)  42.3 us
    reduce_scatter x3, waiting for transfers between devices, local(): lax.psum_scatter(partial_sum.astype(jnp.bfloat16), 'feat', scatter_dimens...  31.5 us
    unnamed x21, local copies, waits for them, and re-layouts  18.7 us
    dot_general x3, matrix products, local(): aggregate = jnp.dot(propagate, joined, preferred_element_type=jnp.float32)  17.8 us
    all_to_all x1, starting transfers between devices, local(): lax.all_to_all(outgoing, 'dom', split_axis=0, concat_axis=0, tiled=True)  13 us
    reduce_sum x1, other arithmetic, local(): jnp.sum(masked, axis=1, keepdims=True)  6.27 us
    convert_element_type x1, other arithmetic, local(): (masked / (1.0 + jnp.sum(masked, axis=1, keepdims=True))).astype(jnp.bflo...  5.98 us
    dot_general x3, matrix products, local(): jnp.dot(support_low, weights[depth], preferred_element_type=jnp.float32)  4.34 us
  transfers between devices with their start and end apart: 4, of which 3 were waited for; matrix products, arithmetic and copies ran while one was open for 19% of the time, Pallas kernels for 0%

commit v1 on v0

v1 whole, which is shorter than its diff:
```python
import functools
import math

import jax
import jax.numpy as jnp
from jax import lax
from jax.experimental import pallas as pl
from jax.experimental.pallas import tpu as pltpu
from jax.sharding import PartitionSpec as P

TILE = 128
BF = jnp.bfloat16
F32 = jnp.float32
MIB = 2**20


def in_vmem(x):
    return pltpu.with_memory_space_constraint(x, pltpu.VMEM)


def nt_dot(a, b):
    return lax.dot_general(a, b, (((1,), (1,)), ((), ())), preferred_element_type=F32)


def pick_kernel(send_hbm, init_hbm, hist_hbm, weight_hbm, out_ref, pack_ref, send_ref, source_ref, weight_ref, sems):
    slots, peers = send_hbm.shape
    width, rows = init_hbm.shape
    layers = hist_hbm.shape[0] + 1
    copies = [pltpu.make_async_copy(init_hbm, source_ref.at[pl.ds(0, width), :], sems.at[0])]
    copies.append(pltpu.make_async_copy(weight_hbm, weight_ref, sems.at[1]))
    for k in range(layers - 1):
        place = source_ref.at[pl.ds((k + 1) * width, width), :]
        copies.append(pltpu.make_async_copy(hist_hbm.at[k], place, sems.at[k + 2]))
    lists_copy = pltpu.make_async_copy(send_hbm, send_ref, sems.at[layers + 1])
    lists_copy.start()
    for copy in copies:
        copy.start()
    lists_copy.wait()
    lists = send_ref[...].T
    spread = jnp.broadcast_to(lists[:, None, :], (peers, slots, slots)).reshape(peers * slots, slots)
    at = lax.broadcasted_iota(jnp.int32, spread.shape, 0) % slots
    lane = lax.broadcasted_iota(jnp.int32, spread.shape, 1)
    index = jnp.sum(jnp.where(at == lane, spread, 0), axis=1, keepdims=True)
    spare = out_ref.shape[1] - layers * width
    out_ref[:, layers * width :] = jnp.zeros((peers * slots, spare), BF)
    cols = weight_ref.shape[2]
    pieces = weight_ref.shape[0] * width // 32
    pack_ref[width:, pieces * cols :] = jnp.zeros((32, rows - pieces * cols), BF)
    copies[1].wait()
    flat = weight_ref[...].reshape(-1, cols)
    for piece in range(pieces):
        pack_ref[width:, piece * cols : (piece + 1) * cols] = flat[piece * 32 : (piece + 1) * 32]
    copies[0].wait()
    pack_ref[:width, :] = source_ref[:width, :]
    for copy in copies[2:]:
        copy.wait()
    step = 128
    for begin in range(0, peers * slots, step):
        node = lax.broadcasted_iota(jnp.int32, (step, rows), 1)
        chosen = jnp.where(node == index[begin : begin + step], 1.0, 0.0).astype(BF)
        out_ref[begin : begin + step, : layers * width] = nt_dot(chosen, source_ref[...]).astype(BF)


def turn_kernel(place_ref, p0, p1, p2, p3, init_ref, weight_ref):
    full = init_ref.shape[1]
    packs = (p0, p1, p2, p3)
    for k, pack in enumerate(packs):
        init_ref[:, k * 64 : (k + 1) * 64] = pack[:64, :].T
    turned = lax.broadcasted_iota(jnp.int32, (full, full), 1) + 64 * place_ref[0]
    turned = jnp.where(turned >= full, turned - full, turned)
    turn = jnp.where(lax.broadcasted_iota(jnp.int32, (full, full), 0) == turned, 1.0, 0.0).astype(BF)
    for k, pack in enumerate(packs):
        flat = jnp.concatenate([pack[64:, j * full : (j + 1) * full] for j in range(6)], axis=0)
        flat = jnp.dot(flat, turn, preferred_element_type=F32).astype(BF)
        for depth in range(3):
            weight_ref[depth, k * 64 : (k + 1) * 64, :] = flat[depth * 64 : (depth + 1) * 64]


def compact_kernel(got_ref, _, out_ref):
    halo = got_ref.shape[0]
    half = halo // 2
    out_ref[:halo, :] = got_ref[:, :128]
    out_ref[halo:, :64] = got_ref[:half, 128:192]
    out_ref[halo:, 64:] = got_ref[half:, 128:192]


def own_kernel(mask_ref, adj_hbm, init_hbm, _, masked_ref, scale_ref, sums_ref, rest_ref, init_ref, sems):
    rows, cols = masked_ref.shape
    chunk = rows // (sems.shape[0] - 1)
    first = pltpu.make_async_copy(init_hbm, init_ref, sems.at[rows // chunk])
    first.start()

    def copy(i):
        part = pl.ds(i * chunk, chunk)
        return pltpu.make_async_copy(adj_hbm.at[part, :], masked_ref.at[part, :], sems.at[i])

    for i in range(rows // chunk):
        copy(i).start()
    first.wait()
    rest_ref[...] = 0.1 * init_ref[...].astype(F32)
    for i in range(rows // TILE):
        if i * TILE % chunk == 0:
            copy(i * TILE // chunk).wait()
        part = pl.ds(i * TILE, TILE)
        total = jnp.zeros((TILE, TILE), F32)
        for t in range(cols // TILE):
            keep = mask_ref[i, t].astype(F32).astype(BF)
            tile = masked_ref[part, t * TILE : (t + 1) * TILE] * keep
            masked_ref[part, t * TILE : (t + 1) * TILE] = tile
            total += tile.astype(F32)
        scale = 0.9 / (1.0 + jnp.sum(total, axis=1, keepdims=True))
        scale_ref[part, :] = jnp.broadcast_to(scale, (TILE, scale_ref.shape[1]))
    block = 1024
    for begin in range(0, rows, block):
        part = pl.ds(begin, block)
        sums_ref[part, :] = jnp.dot(masked_ref[part, :rows], init_ref[...], preferred_element_type=F32)


def finish(depth, acc_ref, scale_ref, rest_ref, weight_ref, made_ref):
    step = 256
    beta = math.log(0.5 / (depth + 1) + 1.0)
    for begin in range(0, acc_ref.shape[0], step):
        part = pl.ds(begin, step)
        scale = jnp.concatenate([scale_ref[part, :]] * 2, axis=1)
        support = acc_ref[part, :] * scale + rest_ref[part, :]
        low = support.astype(BF)
        if depth == 2:
            product = jnp.dot(low, weight_ref[depth, :, :128], preferred_element_type=F32)
            made = jnp.maximum((1.0 - beta) * support[:, :128] + beta * product, 0.0)
            made_ref[:, part] = made.T[:64].astype(BF)
        else:
            product = jnp.dot(low, weight_ref[depth], preferred_element_type=F32)
            made = jnp.maximum((1.0 - beta) * support + beta * product, 0.0).astype(BF)
            made_ref[part, :] = made


def tail_kernel(masked_ref, scale_ref, sums_ref, rest_ref, weight_ref, b0, b1, b2, b3, out_ref, first, second, acc_ref):
    rows, cols = masked_ref.shape
    halo = cols - rows
    half = halo // 2
    packs = (b0, b1, b2, b3)
    block = 1024
    border = jnp.concatenate([pack[:halo, :64] for pack in packs], axis=1)
    first[rows:, :] = jnp.concatenate([pack[:halo, 64:] for pack in packs], axis=1)
    second[rows : rows + half, :] = jnp.concatenate([pack[halo:, :64] for pack in packs], axis=1)
    second[rows + half :, :] = jnp.concatenate([pack[halo:, 64:] for pack in packs], axis=1)
    for begin in range(0, rows, block):
        whole = pl.ds(begin, block)
        more = jnp.dot(masked_ref[whole, rows:], border, preferred_element_type=F32)
        acc_ref[whole, :] = sums_ref[whole, :] + more
    finish(0, acc_ref, scale_ref, rest_ref, weight_ref, first)
    for depth, joined, made_ref in ((1, first, second), (2, second, out_ref)):
        for begin in range(0, rows, block):
            whole = pl.ds(begin, block)
            acc_ref[whole, :] = jnp.dot(masked_ref[whole, :], joined[...], preferred_element_type=F32)
        finish(depth, acc_ref, scale_ref, rest_ref, weight_ref, made_ref)


def ring(x, shift):
    return lax.ppermute(x, "feat", [((i + shift) % 4, i) for i in range(4)])


def local(initial, history, adjacency, tile_mask, send_lists, weights):
    rows, width = initial.shape
    peers, slots = send_lists.shape[1:]
    halo = peers * slots
    cols = rows + halo
    full = weights.shape[2]
    vmem = pl.BlockSpec(memory_space=pltpu.VMEM)
    smem = pl.BlockSpec(memory_space=pltpu.SMEM)
    hbm = pl.BlockSpec(memory_space=pltpu.HBM)
    params = pltpu.CompilerParams
    place = lax.axis_index("feat").astype(jnp.int32).reshape(1)
    layers = weights.shape[0]

    def in_hbm(x):
        return pltpu.with_memory_space_constraint(x, pltpu.HBM)

    outgoing, pack = pl.pallas_call(
        pick_kernel,
        out_shape=[pltpu.VMEM((halo, full), BF), pltpu.VMEM((width + 32, rows), BF)],
        in_specs=[hbm] * 4,
        out_specs=[vmem] * 2,
        scratch_shapes=[
            pltpu.VMEM((slots, peers), jnp.int32),
            pltpu.VMEM((layers * width, rows), BF),
            pltpu.VMEM(weights.shape, BF),
            pltpu.SemaphoreType.DMA((layers + 2,)),
        ],
        compiler_params=params(vmem_limit_bytes=8 * MIB),
        name="pick",
    )(in_hbm(send_lists[0].T), in_hbm(initial.T), in_hbm(jnp.swapaxes(history, 1, 2)), in_hbm(weights))
    packs = [pack] + [ring(pack, shift) for shift in (1, 2, 3)]

    arrived = lax.all_to_all(outgoing.reshape(peers, slots, full), "dom", split_axis=0, concat_axis=0, tiled=True)
    whole_init, turned = pl.pallas_call(
        turn_kernel,
        out_shape=[jax.ShapeDtypeStruct((rows, full), BF), jax.ShapeDtypeStruct((layers, full, full), BF)],
        in_specs=[smem] + [vmem] * 4,
        out_specs=[vmem] * 2,
        compiler_params=params(vmem_limit_bytes=8 * MIB),
        cost_estimate=pl.CostEstimate(flops=8_000_000_000, bytes_accessed=4 * rows * full, transcendentals=0),
        name="turn",
    )(place, *[in_vmem(p) for p in packs])

    border = pl.pallas_call(
        compact_kernel,
        out_shape=pltpu.VMEM((halo + halo // 2, 128), BF),
        in_specs=[vmem, hbm],
        out_specs=vmem,
        compiler_params=params(vmem_limit_bytes=2 * MIB),
        name="compact",
    )(in_vmem(arrived.reshape(halo, full)), in_hbm(whole_init))
    borders = [border] + [ring(border, shift) for shift in (1, 2, 3)]

    masked, scale, sums, rest = pl.pallas_call(
        own_kernel,
        out_shape=[
            pltpu.VMEM((rows, cols), BF),
            pltpu.VMEM((rows, 128), F32),
            pltpu.VMEM((rows, full), F32),
            pltpu.VMEM((rows, full), F32),
        ],
        in_specs=[smem, hbm, hbm, vmem],
        out_specs=[vmem] * 4,
        scratch_shapes=[pltpu.VMEM((rows, full), BF), pltpu.SemaphoreType.DMA((9,))],
        compiler_params=params(vmem_limit_bytes=8 * MIB),
        cost_estimate=pl.CostEstimate(flops=4 * rows * rows * full, bytes_accessed=2 * rows * cols, transcendentals=0),
        name="own",
    )(tile_mask, in_hbm(adjacency), in_hbm(whole_init), in_vmem(border))

    out = pl.pallas_call(
        tail_kernel,
        out_shape=jax.ShapeDtypeStruct((width, rows), BF),
        in_specs=[vmem] * 9,
        out_specs=vmem,
        scratch_shapes=[pltpu.VMEM((cols, full), BF), pltpu.VMEM((cols, full), BF), pltpu.VMEM((rows, full), F32)],
        compiler_params=params(vmem_limit_bytes=12 * MIB),
        name="tail",
    )(*[in_vmem(x) for x in (masked, scale, sums, rest, turned, *borders)])
    return out.T


def solution(mesh):
    placed = (
        P("dom", "feat"),
        P(None, "dom", "feat"),
        P("dom", None),
        P("dom", None),
        P("dom", None, None),
        P(None, "feat", None),
    )
    return jax.shard_map(
        local, mesh=mesh, in_specs=placed, out_specs=P("dom", "feat"), check_vma=False
    )
```

time: 165 us -> 57.3 us (0.35)
  blocking collectives: 42.3 us -> 0 us
  local copies, waits for them, and re-layouts: 23.3 us -> 0.97 us
  matrix products: 22.1 us -> 0 us
  Pallas kernels: 0 us -> 20.3 us
  other arithmetic: 17.5 us -> 0 us
  waiting for transfers between devices: 31.6 us -> 14.6 us
  between operations: 13.3 us -> 0.06 us
  starting transfers between devices: 13.1 us -> 21.1 us
    all_to_all x2 -> x0, blocking collectives: 42.3 us -> none  [local(): lax.all_to_all(outgoing, 'dom', split_axis=0, concat_axis=0, tiled=True)]
    reduce_scatter x3 -> x0, waiting for transfers between devices: 31.5 us -> none  [local(): lax.psum_scatter(partial_sum.astype(jnp.bfloat16), 'feat', scatter_dimens...]
    dot_general x6 -> x0, matrix products: 22.1 us -> none  [the longest x3 17.8 us: local(): aggregate = jnp.dot(propagate, joined, preferred_element_type=jnp.float32)]
    pallas_call x0 -> x5, Pallas kernels: none -> 20.3 us  [the longest x1 8.4 us: local(): pl.pallas_call(tail_kernel, out_shape=jax.ShapeDtypeStruct((width, rows),...]
    unnamed x21 -> x4, local copies, waits for them, and re-layouts: 18.7 us -> 0.97 us
    ppermute x0 -> x6, waiting for transfers between devices: none -> 10.6 us  [ring(): return lax.ppermute(x, 'feat', [((i + shift) % 4, i) for i in range(4)])]
    convert_element_type x5 -> x0, other arithmetic: 10.5 us -> none  [the longest x1 5.98 us: local(): (masked / (1.0 + jnp.sum(masked, axis=1, keepdims=True))).astype(jnp.bflo...]
    ppermute x0 -> x6, starting transfers between devices: none -> 8.13 us  [ring(): return lax.ppermute(x, 'feat', [((i + shift) % 4, i) for i in range(4)])]
  transfers between devices with their start and end apart: 4 -> 7, of which waited for: 3 -> 4; matrix products, arithmetic and copies ran while one was open for 19% -> 0% of each run, Pallas kernels for 0% -> 15%
where the time goes in v1:
time: 57.3 us; the launch traced here: 57.1 us
  starting transfers between devices  21.1 us (37%)
  Pallas kernels  20.3 us (35%)
  waiting for transfers between devices  14.6 us (25%)
  local copies, waits for them, and re-layouts  0.97 us (2%)
    all_to_all x1, starting transfers between devices, local(): lax.all_to_all(outgoing.reshape(peers, slots, full), 'dom', split_axis=0,...  13 us
    ppermute x6, waiting for transfers between devices, ring(): return lax.ppermute(x, 'feat', [((i + shift) % 4, i) for i in range(4)])  10.6 us
    pallas_call x1, Pallas kernels, local(): pl.pallas_call(tail_kernel, out_shape=jax.ShapeDtypeStruct((width, rows),...  8.4 us
    ppermute x6, starting transfers between devices, ring(): return lax.ppermute(x, 'feat', [((i + shift) % 4, i) for i in range(4)])  8.13 us
    pallas_call x1, Pallas kernels, local(): pl.pallas_call(own_kernel, out_shape=[pltpu.VMEM((rows, cols), BF), pltpu...  7.47 us
    all_to_all x1, waiting for transfers between devices, local(): lax.all_to_all(outgoing.reshape(peers, slots, full), 'dom', split_axis=0,...  4.05 us
    pallas_call x1, Pallas kernels, local(): pl.pallas_call(pick_kernel, out_shape=[pltpu.VMEM((halo, full), BF), pltp...  3.15 us
    pallas_call x1, Pallas kernels, local(): pl.pallas_call(turn_kernel, out_shape=[jax.ShapeDtypeStruct((rows, full),...  1.2 us
  transfers between devices with their start and end apart: 7, of which 4 were waited for; matrix products, arithmetic and copies ran while one was open for 0% of the time, Pallas kernels for 15%

profile of v1, /device:TPU:1, one launch (start us, length us, event | category | flops | bytes accessed | tf_op | source)
XLA Modules:
  0.0 57.1 jit_solution(18402331271268275443)
XLA Ops:
  0.0 3.1 %pick.1 = (bf16[512,256]{1,0:T(8,128)(2,1)}, bf16[96,2048]{1,0:T(8,128)(2,1)S(1)}) custom-call(s32[8,64]{1,0:T(8,128)} %bitcast.12, bf16[64,2048]{1,0:T(8,128)(2,1)} %bitcast.11, bf16[2,64,2048]{2,1,0:T(8,128)(2,1)} %bitcast.10, bf16[3,64,256]{2,1,0:T(8,128)(2,1)} %weight_hbm.1), custom_call_target="tpu_custom_call" | custom-call | tf_op jit(solution)/shard_map/pick/pallas_call | solution.py:179
  3.2 3.6 %collective-permute-start = (bf16[96,2048]{1,0:T(8,128)(2,1)S(1)}, bf16[96,2048]{1,0:T(8,128)(2,1)S(1)}, u32[]{:S(2)}, u32[]{:S(2)}) collective-permute-start(bf16[96,2048]{1,0:T(8,128)(2,1)S(1)} %get-tuple-element.13.p0), channel_id=1, source_target_pairs={{1,0},{2,1},{3,2},{0,3},{5,4},{6,5},{7,6},{4,7},{9,8},{10,9},{11,1... | collective-permute-start | bytes 1179656 | tf_op jit(solution)/shard_map/ppermute | solution.py:160
  6.8 0.4 collective-permute-start.1
  7.1 0.7 %collective-permute-start.2 = (bf16[96,2048]{1,0:T(8,128)(2,1)S(1)}, bf16[96,2048]{1,0:T(8,128)(2,1)S(1)}, u32[]{:S(2)}, u32[]{:S(2)}) collective-permute-start(bf16[96,2048]{1,0:T(8,128)(2,1)S(1)} %get-tuple-element.13.p0), channel_id=1, source_target_pairs={{3,0},{0,1},{1,2},{2,3},{7,4},{4,5},{5,6},{6,7},{11,8},{8,9},{9,10... | collective-permute-start | bytes 1179656 | tf_op jit(solution)/shard_map/ppermute | solution.py:160
  7.8 13.0 %all-to-all-start = ((bf16[64,8,256]{2,1,0:T(8,128)(2,1)}), bf16[64,8,256]{2,1,0:T(8,128)(2,1)S(1)}, u32[]{:S(2)}, u32[]{:S(2)}) async-start(bf16[64,8,256]{2,1,0:T(8,128)(2,1)} %bitcast.5), calls=%async_computation | async-start | bytes 524288 | tf_op jit(solution)/shard_map/all_to_all | solution.py:195
  20.8 2.0 %collective-permute-done.p1 = bf16[96,2048]{1,0:T(8,128)(2,1)S(1)} collective-permute-done((bf16[96,2048]{1,0:T(8,128)(2,1)S(1)}, bf16[96,2048]{1,0:T(8,128)(2,1)S(1)}, u32[]{:S(2)}, u32[]{:S(2)}) %collective-permute-start) | collective-permute-done | bytes 393248 | tf_op jit(solution)/shard_map/ppermute | solution.py:160
  22.8 0.0 collective-permute-done.1.p2
  22.8 4.9 %collective-permute-done.2.p3 = bf16[96,2048]{1,0:T(8,128)(2,1)S(1)} collective-permute-done((bf16[96,2048]{1,0:T(8,128)(2,1)S(1)}, bf16[96,2048]{1,0:T(8,128)(2,1)S(1)}, u32[]{:S(2)}, u32[]{:S(2)}) %collective-permute-start.2) | collective-permute-done | bytes 393248 | tf_op jit(solution)/shard_map/ppermute | solution.py:160
  27.7 0.0 copy-start.1
  27.7 1.2 %turn.1 = (bf16[2048,256]{1,0:T(8,128)(2,1)S(1)}, bf16[3,256,256]{2,1,0:T(8,128)(2,1)S(1)}) custom-call(s32[1]{0:T(128)} %bitcast.place_ref, bf16[96,2048]{1,0:T(8,128)(2,1)S(1)} %get-tuple-element.13.p0, bf16[96,2048]{1,0:T(8,128)(2,1)S(1)} %collective-permute-done.p1, bf16[96,2048]{1,0:T(8,128)(2,1)S(1)} %collective-permute-done.1.p2, ...), custom_call_target="tpu_custom_call" | custom-call | flops 8000000000 | bytes 2097152 | tf_op jit(solution)/shard_map/turn/pallas_call | solution.py:196
  29.0 0.0 copy-start
  29.0 1.0 %copy-done = bf16[2048,256]{1,0:T(8,128)(2,1)} copy-done((bf16[2048,256]{1,0:T(8,128)(2,1)}, bf16[2048,256]{1,0:T(8,128)(2,1)S(1)}, u32[]{:S(2)}) %copy-start) | copy-done | bytes 1048600
  29.9 4.1 %all-to-all-done = bf16[64,8,256]{2,1,0:T(8,128)(2,1)S(1)} async-done(((bf16[64,8,256]{2,1,0:T(8,128)(2,1)}), bf16[64,8,256]{2,1,0:T(8,128)(2,1)S(1)}, u32[]{:S(2)}, u32[]{:S(2)}) %all-to-all-start) | async-done | bytes 262176 | tf_op jit(solution)/shard_map/all_to_all | solution.py:195
  34.0 0.1 compact.1._.b0
  34.1 2.1 %collective-permute-start.3 = (bf16[768,128]{1,0:T(8,128)(2,1)S(1)}, bf16[768,128]{1,0:T(8,128)(2,1)S(1)}, u32[]{:S(2)}, u32[]{:S(2)}) collective-permute-start(bf16[768,128]{1,0:T(8,128)(2,1)S(1)} %compact.1._.b0), channel_id=1, source_target_pairs={{1,0},{2,1},{3,2},{0,3},{5,4},{6,5},{7,6},{4,7},{9,8},{10,9},{11,1... | collective-permute-start | bytes 589832 | tf_op jit(solution)/shard_map/ppermute | solution.py:160
  36.2 1.4 %collective-permute-start.4 = (bf16[768,128]{1,0:T(8,128)(2,1)S(1)}, bf16[768,128]{1,0:T(8,128)(2,1)S(1)}, u32[]{:S(2)}, u32[]{:S(2)}) collective-permute-start(bf16[768,128]{1,0:T(8,128)(2,1)S(1)} %compact.1._.b0), channel_id=1, source_target_pairs={{2,0},{3,1},{0,2},{1,3},{6,4},{7,5},{4,6},{5,7},{10,8},{11,9},{8,1... | collective-permute-start | bytes 589832 | tf_op jit(solution)/shard_map/ppermute | solution.py:160
  37.6 0.0 collective-permute-start.5
  37.6 0.0 copy-done.1
  37.6 7.5 %own.1 = (bf16[2048,2560]{1,0:T(8,128)(2,1)S(1)}, f32[2048,128]{1,0:T(8,128)S(1)}, f32[2048,256]{1,0:T(8,128)S(1)}, f32[2048,256]{1,0:T(8,128)S(1)}) custom-call(s32[16,20]{1,0:T(8,128)S(1)} %copy-done.1, bf16[2048,2560]{1,0:T(8,128)(2,1)} %adj_hbm.1, bf16[2048,256]{1,0:T(8,128)(2,1)} %copy-done, bf16[768,128]{1,0:T(8,128)(2,1)S(1)} %compact.1._.b0), custom_call_target="tpu_custom_call" | custom-call | flops 4294967296 | bytes 10485760 | tf_op jit(solution)/shard_map/own/pallas_call | solution.py:216
  45.0 0.0 collective-permute-done.3.b1
  45.0 0.0 collective-permute-done.4.b2
  45.1 3.7 %collective-permute-done.5.b3 = bf16[768,128]{1,0:T(8,128)(2,1)S(1)} collective-permute-done((bf16[768,128]{1,0:T(8,128)(2,1)S(1)}, bf16[768,128]{1,0:T(8,128)(2,1)S(1)}, u32[]{:S(2)}, u32[]{:S(2)}) %collective-permute-start.5) | collective-permute-done | bytes 196640 | tf_op jit(solution)/shard_map/ppermute | solution.py:160
  48.7 8.4 %tail.1 = bf16[64,2048]{1,0:T(8,128)(2,1)} custom-call(bf16[2048,2560]{1,0:T(8,128)(2,1)S(1)} %get-tuple-element.16.masked_ref, f32[2048,128]{1,0:T(8,128)S(1)} %get-tuple-element.17.scale_ref, f32[2048,256]{1,0:T(8,128)S(1)} %get-tuple-element.18.sums_ref, f32[2048,256]{1,0:T(8,128)S(1)} %get-tuple-element.19.rest_ref, ...), custom_call_target="tpu_custom_call" | custom-call | tf_op jit(solution)/shard_map/tail/pallas_call | solution.py:232
Async XLA Ops:
  3.2 19.7 %collective-permute-start = (bf16[96,2048]{1,0:T(8,128)(2,1)S(1)}, bf16[96,2048]{1,0:T(8,128)(2,1)S(1)}, u32[]{:S(2)}, u32[]{:S(2)}) collective-permute-start(bf16[96,2048]{1,0:T(8,128)(2,1)S(1)} %get-tuple-element.13.p0), channel_id=1, source_target_pairs={{1,0},{2,1},{3,2},{0,3},{5,4},{6,5},{7,6},{4,7},{9,8},{10,9},{11,1... | collective-permute-start | bytes 1179656 | tf_op jit(solution)/shard_map/ppermute | solution.py:160
  6.8 16.0 %collective-permute-start.1 = (bf16[96,2048]{1,0:T(8,128)(2,1)S(1)}, bf16[96,2048]{1,0:T(8,128)(2,1)S(1)}, u32[]{:S(2)}, u32[]{:S(2)}) collective-permute-start(bf16[96,2048]{1,0:T(8,128)(2,1)S(1)} %get-tuple-element.13.p0), channel_id=1, source_target_pairs={{2,0},{3,1},{0,2},{1,3},{6,4},{7,5},{4,6},{5,7},{10,8},{11,9},{8,1... | collective-permute-start | bytes 1179656 | tf_op jit(solution)/shard_map/ppermute | solution.py:160
  7.1 20.6 %collective-permute-start.2 = (bf16[96,2048]{1,0:T(8,128)(2,1)S(1)}, bf16[96,2048]{1,0:T(8,128)(2,1)S(1)}, u32[]{:S(2)}, u32[]{:S(2)}) collective-permute-start(bf16[96,2048]{1,0:T(8,128)(2,1)S(1)} %get-tuple-element.13.p0), channel_id=1, source_target_pairs={{3,0},{0,1},{1,2},{2,3},{7,4},{4,5},{5,6},{6,7},{11,8},{8,9},{9,10... | collective-permute-start | bytes 1179656 | tf_op jit(solution)/shard_map/ppermute | solution.py:160
  7.8 26.2 %all-to-all-start = ((bf16[64,8,256]{2,1,0:T(8,128)(2,1)}), bf16[64,8,256]{2,1,0:T(8,128)(2,1)S(1)}, u32[]{:S(2)}, u32[]{:S(2)}) async-start(bf16[64,8,256]{2,1,0:T(8,128)(2,1)} %bitcast.5), calls=%async_computation | async-start | bytes 524288 | tf_op jit(solution)/shard_map/all_to_all | solution.py:195
  27.7 9.8 %copy-start.1 = (s32[16,20]{1,0:T(8,128)S(1)}, s32[16,20]{1,0:T(8,128)}, u32[]{:S(2)}) copy-start(s32[16,20]{1,0:T(8,128)} %mask_ref.1) | copy-start | bytes 3844
  29.0 1.0 %copy-start = (bf16[2048,256]{1,0:T(8,128)(2,1)}, bf16[2048,256]{1,0:T(8,128)(2,1)S(1)}, u32[]{:S(2)}) copy-start(bf16[2048,256]{1,0:T(8,128)(2,1)S(1)} %get-tuple-element.14._.init_hbm) | copy-start | bytes 3145732
  34.1 10.9 %collective-permute-start.3 = (bf16[768,128]{1,0:T(8,128)(2,1)S(1)}, bf16[768,128]{1,0:T(8,128)(2,1)S(1)}, u32[]{:S(2)}, u32[]{:S(2)}) collective-permute-start(bf16[768,128]{1,0:T(8,128)(2,1)S(1)} %compact.1._.b0), channel_id=1, source_target_pairs={{1,0},{2,1},{3,2},{0,3},{5,4},{6,5},{7,6},{4,7},{9,8},{10,9},{11,1... | collective-permute-start | bytes 589832 | tf_op jit(solution)/shard_map/ppermute | solution.py:160
  36.2 8.9 %collective-permute-start.4 = (bf16[768,128]{1,0:T(8,128)(2,1)S(1)}, bf16[768,128]{1,0:T(8,128)(2,1)S(1)}, u32[]{:S(2)}, u32[]{:S(2)}) collective-permute-start(bf16[768,128]{1,0:T(8,128)(2,1)S(1)} %compact.1._.b0), channel_id=1, source_target_pairs={{2,0},{3,1},{0,2},{1,3},{6,4},{7,5},{4,6},{5,7},{10,8},{11,9},{8,1... | collective-permute-start | bytes 589832 | tf_op jit(solution)/shard_map/ppermute | solution.py:160
  37.6 11.2 %collective-permute-start.5 = (bf16[768,128]{1,0:T(8,128)(2,1)S(1)}, bf16[768,128]{1,0:T(8,128)(2,1)S(1)}, u32[]{:S(2)}, u32[]{:S(2)}) collective-permute-start(bf16[768,128]{1,0:T(8,128)(2,1)S(1)} %compact.1._.b0), channel_id=1, source_target_pairs={{3,0},{0,1},{1,2},{2,3},{7,4},{4,5},{5,6},{6,7},{11,8},{8,9},{9,10... | collective-permute-start | bytes 589832 | tf_op jit(solution)/shard_map/ppermute | solution.py:160

commit v2 on v1

--- a/solution.py
+++ b/solution.py
@@ -22,7 +22,7 @@
     return lax.dot_general(a, b, (((1,), (1,)), ((), ())), preferred_element_type=F32)
 
 
-def pick_kernel(send_hbm, init_hbm, hist_hbm, weight_hbm, out_ref, pack_ref, send_ref, source_ref, weight_ref, sems):
+def pick_kernel(send_hbm, init_hbm, hist_hbm, weight_hbm, out_ref, pack_a, pack_b, send_ref, chosen_ref, source_ref, weight_ref, sems):
     slots, peers = send_hbm.shape
     width, rows = init_hbm.shape
     layers = hist_hbm.shape[0] + 1
@@ -41,54 +41,57 @@
     at = lax.broadcasted_iota(jnp.int32, spread.shape, 0) % slots
     lane = lax.broadcasted_iota(jnp.int32, spread.shape, 1)
     index = jnp.sum(jnp.where(at == lane, spread, 0), axis=1, keepdims=True)
+    step = 64
+    for begin in range(0, peers * slots, step):
+        node = lax.broadcasted_iota(jnp.int32, (step, rows), 1)
+        chosen_ref[begin : begin + step, :] = jnp.where(node == index[begin : begin + step], 1.0, 0.0).astype(BF)
     spare = out_ref.shape[1] - layers * width
     out_ref[:, layers * width :] = jnp.zeros((peers * slots, spare), BF)
-    cols = weight_ref.shape[2]
-    pieces = weight_ref.shape[0] * width // 32
-    pack_ref[width:, pieces * cols :] = jnp.zeros((32, rows - pieces * cols), BF)
+    full = weight_ref.shape[2]
+    parts = rows // full
     copies[1].wait()
-    flat = weight_ref[...].reshape(-1, cols)
-    for piece in range(pieces):
-        pack_ref[width:, piece * cols : (piece + 1) * cols] = flat[piece * 32 : (piece + 1) * 32]
+    flat = weight_ref[...].reshape(-1, full)
+    half = flat.shape[0] // 2
+    for n, pack_ref in enumerate((pack_a, pack_b)):
+        pack_ref[parts // 2 * width :, :] = flat[n * half : (n + 1) * half]
     copies[0].wait()
-    pack_ref[:width, :] = source_ref[:width, :]
+    for n, pack_ref in enumerate((pack_a, pack_b)):
+        for j in range(parts // 2):
+            begin = (n * parts // 2 + j) * full
+            pack_ref[j * width : (j + 1) * width, :] = source_ref[:width, begin : begin + full]
     for copy in copies[2:]:
         copy.wait()
-    step = 128
-    for begin in range(0, peers * slots, step):
-        node = lax.broadcasted_iota(jnp.int32, (step, rows), 1)
-        chosen = jnp.where(node == index[begin : begin + step], 1.0, 0.0).astype(BF)
-        out_ref[begin : begin + step, : layers * width] = nt_dot(chosen, source_ref[...]).astype(BF)
-
-
-def turn_kernel(place_ref, p0, p1, p2, p3, init_ref, weight_ref):
-    full = init_ref.shape[1]
-    packs = (p0, p1, p2, p3)
-    for k, pack in enumerate(packs):
-        init_ref[:, k * 64 : (k + 1) * 64] = pack[:64, :].T
-    turned = lax.broadcasted_iota(jnp.int32, (full, full), 1) + 64 * place_ref[0]
-    turned = jnp.where(turned >= full, turned - full, turned)
-    turn = jnp.where(lax.broadcasted_iota(jnp.int32, (full, full), 0) == turned, 1.0, 0.0).astype(BF)
-    for k, pack in enumerate(packs):
-        flat = jnp.concatenate([pack[64:, j * full : (j + 1) * full] for j in range(6)], axis=0)
-        flat = jnp.dot(flat, turn, preferred_element_type=F32).astype(BF)
-        for depth in range(3):
-            weight_ref[depth, k * 64 : (k + 1) * 64, :] = flat[depth * 64 : (depth + 1) * 64]
-
-
-def compact_kernel(got_ref, _, out_ref):
-    halo = got_ref.shape[0]
-    half = halo // 2
-    out_ref[:halo, :] = got_ref[:, :128]
-    out_ref[halo:, :64] = got_ref[:half, 128:192]
-    out_ref[halo:, 64:] = got_ref[half:, 128:192]
-
-
-def own_kernel(mask_ref, adj_hbm, init_hbm, _, masked_ref, scale_ref, sums_ref, rest_ref, init_ref, sems):
+    out_ref[:, : layers * width] = nt_dot(chosen_ref[...], source_ref[...]).astype(BF)
+
+
+def split_kernel(core_ref, got_ref, mine_ref, other_ref):
+    chips = got_ref.shape[0]
+    full = got_ref.shape[2]
+    low, high = got_ref[:, :8, :], got_ref[:, 8:, :]
+    first = core_ref[0] == 0
+    mine_ref[...] = jnp.where(first, low, high).reshape(chips * 8, full)
+    other_ref[...] = jnp.where(first, high, low).reshape(chips * 8, full)
+
+
+def merge_kernel(core_ref, mine_ref, other_ref, out_ref):
+    count, full = mine_ref.shape
+    chips = count // 8
+    halo = 2 * count
+    first = core_ref[0] == 0
+    mine = mine_ref[...].reshape(chips, 8, full)
+    other = other_ref[...].reshape(chips, 8, full)
+    low, high = jnp.where(first, mine, other), jnp.where(first, other, mine)
+    got = jnp.concatenate([low, high], axis=1).reshape(halo, full)
+    out_ref[:halo, :] = got[:, :128]
+    out_ref[halo:, :64] = got[:count, 128:192]
+    out_ref[halo:, 64:] = got[count:, 128:192]
+
+
+def prep_kernel(mask_hbm, adj_hbm, _, __, ___, _a, _b, masked_ref, scale_ref, mask_ref, sems):
     rows, cols = masked_ref.shape
     chunk = rows // (sems.shape[0] - 1)
-    first = pltpu.make_async_copy(init_hbm, init_ref, sems.at[rows // chunk])
-    first.start()
+    mask_copy = pltpu.make_async_copy(mask_hbm, mask_ref, sems.at[rows // chunk])
+    mask_copy.start()
 
     def copy(i):
         part = pl.ds(i * chunk, chunk)
@@ -96,8 +99,7 @@
 
     for i in range(rows // chunk):
         copy(i).start()
-    first.wait()
-    rest_ref[...] = 0.1 * init_ref[...].astype(F32)
+    mask_copy.wait()
     for i in range(rows // TILE):
         if i * TILE % chunk == 0:
             copy(i * TILE // chunk).wait()
@@ -110,10 +112,34 @@
             total += tile.astype(F32)
         scale = 0.9 / (1.0 + jnp.sum(total, axis=1, keepdims=True))
         scale_ref[part, :] = jnp.broadcast_to(scale, (TILE, scale_ref.shape[1]))
+
+
+def own_kernel(place_ref, masked_ref, a0, a1, a2, a3, b0, b1, b2, b3, sums_ref, rest_ref, weight_ref, init_ref):
+    rows = masked_ref.shape[0]
+    full = init_ref.shape[1]
+    width = full // 4
+    parts = rows // full
+    packs = ((a0, a1, a2, a3), (b0, b1, b2, b3))
+    turned = lax.broadcasted_iota(jnp.int32, (full, full), 1) + width * place_ref[0]
+    turned = jnp.where(turned >= full, turned - full, turned)
+    turn = jnp.where(lax.broadcasted_iota(jnp.int32, (full, full), 0) == turned, 1.0, 0.0).astype(BF)
+    for n, group in enumerate(packs):
+        for j in range(parts // 2):
+            piece = jnp.concatenate([pack[j * width : (j + 1) * width, :] for pack in group], axis=0)
+            begin = (n * parts // 2 + j) * full
+            init_ref[begin : begin + full, :] = piece.T
+    begin = parts // 2 * width
+    layers = weight_ref.shape[0]
+    for k in range(4):
+        flat = jnp.concatenate([group[k][begin:, :] for group in packs], axis=0)
+        flat = jnp.dot(flat, turn, preferred_element_type=F32).astype(BF)
+        for depth in range(layers):
+            weight_ref[depth, k * width : (k + 1) * width, :] = flat[depth * width : (depth + 1) * width]
     block = 1024
     for begin in range(0, rows, block):
         part = pl.ds(begin, block)
         sums_ref[part, :] = jnp.dot(masked_ref[part, :rows], init_ref[...], preferred_element_type=F32)
+    rest_ref[...] = 0.1 * init_ref[...].astype(F32)
 
 
 def finish(depth, acc_ref, scale_ref, rest_ref, weight_ref, made_ref):
@@ -176,13 +202,14 @@
     def in_hbm(x):
         return pltpu.with_memory_space_constraint(x, pltpu.HBM)
 
-    outgoing, pack = pl.pallas_call(
+    outgoing, pack_a, pack_b = pl.pallas_call(
         pick_kernel,
-        out_shape=[pltpu.VMEM((halo, full), BF), pltpu.VMEM((width + 32, rows), BF)],
+        out_shape=[pltpu.VMEM((halo, full), BF)] + [pltpu.VMEM(((rows // full + layers) * width // 2, full), BF)] * 2,
         in_specs=[hbm] * 4,
-        out_specs=[vmem] * 2,
+        out_specs=[vmem] * 3,
         scratch_shapes=[
             pltpu.VMEM((slots, peers), jnp.int32),
+            pltpu.VMEM((halo, rows), BF),
             pltpu.VMEM((layers * width, rows), BF),
             pltpu.VMEM(weights.shape, BF),
             pltpu.SemaphoreType.DMA((layers + 2,)),
@@ -190,44 +217,61 @@
         compiler_params=params(vmem_limit_bytes=8 * MIB),
         name="pick",
     )(in_hbm(send_lists[0].T), in_hbm(initial.T), in_hbm(jnp.swapaxes(history, 1, 2)), in_hbm(weights))
-    packs = [pack] + [ring(pack, shift) for shift in (1, 2, 3)]
-
-    arrived = lax.all_to_all(outgoing.reshape(peers, slots, full), "dom", split_axis=0, concat_axis=0, tiled=True)
-    whole_init, turned = pl.pallas_call(
-        turn_kernel,
-        out_shape=[jax.ShapeDtypeStruct((rows, full), BF), jax.ShapeDtypeStruct((layers, full, full), BF)],
-        in_specs=[smem] + [vmem] * 4,
+    a1, a3 = ring(pack_a, 1), ring(pack_a, 3)
+    b1, b3 = ring(pack_b, 1), ring(pack_b, 3)
+    packs = [pack_a, a1, ring(a1, 1), a3, pack_b, b1, ring(b3, 3), b3]
+
+    cores = 2
+    chips = peers // cores
+    core = lax.rem(lax.axis_index("dom"), cores).astype(jnp.int32).reshape(1)
+    groups = [[chip * cores + c for chip in range(chips)] for c in range(cores)]
+    arrived = lax.all_to_all(
+        outgoing.reshape(chips, cores * slots, full), "dom", split_axis=0, concat_axis=0, tiled=True, axis_index_groups=groups
+    )
+    mine, other = pl.pallas_call(
+        split_kernel,
+        out_shape=[pltpu.VMEM((halo // 2, full), BF)] * 2,
+        in_specs=[smem, vmem],
         out_specs=[vmem] * 2,
-        compiler_params=params(vmem_limit_bytes=8 * MIB),
-        cost_estimate=pl.CostEstimate(flops=8_000_000_000, bytes_accessed=4 * rows * full, transcendentals=0),
-        name="turn",
-    )(place, *[in_vmem(p) for p in packs])
-
+        compiler_params=params(vmem_limit_bytes=4 * MIB),
+        name="split",
+    )(core, in_vmem(arrived))
+    swap = [(i, i ^ 1) for i in range(peers)]
     border = pl.pallas_call(
-        compact_kernel,
+        merge_kernel,
         out_shape=pltpu.VMEM((halo + halo // 2, 128), BF),
-        in_specs=[vmem, hbm],
+        in_specs=[smem, vmem, vmem],
         out_specs=vmem,
-        compiler_params=params(vmem_limit_bytes=2 * MIB),
-        name="compact",
-    )(in_vmem(arrived.reshape(halo, full)), in_hbm(whole_init))
+        compiler_params=params(vmem_limit_bytes=4 * MIB),
+        name="merge",
+    )(core, in_vmem(mine), in_vmem(lax.ppermute(other, "dom", swap)))
     borders = [border] + [ring(border, shift) for shift in (1, 2, 3)]
 
-    masked, scale, sums, rest = pl.pallas_call(
+    masked, scale = pl.pallas_call(
+        prep_kernel,
+        out_shape=[pltpu.VMEM((rows, cols), BF), pltpu.VMEM((rows, 128), F32)],
+        in_specs=[hbm, hbm] + [vmem] * 5,
+        out_specs=[vmem] * 2,
+        scratch_shapes=[pltpu.SMEM(tile_mask.shape, jnp.int32), pltpu.SemaphoreType.DMA((9,))],
+        compiler_params=params(vmem_limit_bytes=4 * MIB),
+        cost_estimate=pl.CostEstimate(flops=4_300_000_000, bytes_accessed=1000, transcendentals=0),
+        name="prep",
+    )(in_hbm(tile_mask), in_hbm(adjacency), in_vmem(border), *[in_vmem(packs[k]) for k in (2, 6, 3, 5)])
+
+    sums, rest, turned = pl.pallas_call(
         own_kernel,
         out_shape=[
-            pltpu.VMEM((rows, cols), BF),
-            pltpu.VMEM((rows, 128), F32),
             pltpu.VMEM((rows, full), F32),
             pltpu.VMEM((rows, full), F32),
+            pltpu.VMEM((layers, full, full), BF),
         ],
-        in_specs=[smem, hbm, hbm, vmem],
-        out_specs=[vmem] * 4,
-        scratch_shapes=[pltpu.VMEM((rows, full), BF), pltpu.SemaphoreType.DMA((9,))],
+        in_specs=[smem] + [vmem] * 9,
+        out_specs=[vmem] * 3,
+        scratch_shapes=[pltpu.VMEM((rows, full), BF)],
         compiler_params=params(vmem_limit_bytes=8 * MIB),
-        cost_estimate=pl.CostEstimate(flops=4 * rows * rows * full, bytes_accessed=2 * rows * cols, transcendentals=0),
+        cost_estimate=pl.CostEstimate(flops=1000, bytes_accessed=1000, transcendentals=0),
         name="own",
-    )(tile_mask, in_hbm(adjacency), in_hbm(whole_init), in_vmem(border))
+    )(place, in_vmem(masked), *[in_vmem(p) for p in packs])
 
     out = pl.pallas_call(
         tail_kernel,

time: 57.3 us -> 53.9 us (0.941)
  waiting for transfers between devices: 14.6 us -> 7.82 us
  starting transfers between devices: 21.1 us -> 27.2 us
  Pallas kernels: 20.3 us -> 18.6 us
  local copies, waits for them, and re-layouts: 0.97 us -> 0 us
    ppermute x6 -> x9, waiting for transfers between devices: 10.6 us -> 4.77 us  [ring(): return lax.ppermute(x, 'feat', [((i + shift) % 4, i) for i in range(4)])]
    ppermute x6 -> x9, starting transfers between devices: 8.13 us -> 12.8 us  [ring(): return lax.ppermute(x, 'feat', [((i + shift) % 4, i) for i in range(4)])]
    ppermute x0 -> x1, starting transfers between devices: none -> 2.53 us  [local(): lax.ppermute(other, 'dom', swap)]
    pallas_call x4 -> x5, Pallas kernels: 11.9 us -> 9.92 us  [the longest x1 4.46 us: local(): pl.pallas_call(prep_kernel, out_shape=[pltpu.VMEM((rows, cols), BF), pltp...]
    all_to_all x1, waiting for transfers between devices: 4.05 us -> 2.06 us  [local(): lax.all_to_all(outgoing.reshape(chips, cores * slots, full), 'dom', split...]
    all_to_all x1, starting transfers between devices: 13 us -> 11.9 us  [local(): lax.all_to_all(outgoing.reshape(chips, cores * slots, full), 'dom', split...]
    ppermute x0 -> x1, waiting for transfers between devices: none -> 0.99 us  [local(): lax.ppermute(other, 'dom', swap)]
    unnamed x4 -> x0, local copies, waits for them, and re-layouts: 0.97 us -> none
  transfers between devices with their start and end apart: 7 -> 11, of which waited for: 4 -> 4; matrix products, arithmetic and copies ran while one was open for 0% -> 0% of each run, Pallas kernels for 15% -> 13%
where the time goes in v2:
time: 53.9 us; the launch traced here: 53.6 us
  starting transfers between devices  27.2 us (50%)
  Pallas kernels  18.6 us (35%)
  waiting for transfers between devices  7.82 us (15%)
    ppermute x9, starting transfers between devices, ring(): return lax.ppermute(x, 'feat', [((i + shift) % 4, i) for i in range(4)])  12.8 us
    all_to_all x1, starting transfers between devices, local(): lax.all_to_all(outgoing.reshape(chips, cores * slots, full), 'dom', split...  11.9 us
    pallas_call x1, Pallas kernels, local(): pl.pallas_call(tail_kernel, out_shape=jax.ShapeDtypeStruct((width, rows),...  8.65 us
    ppermute x9, waiting for transfers between devices, ring(): return lax.ppermute(x, 'feat', [((i + shift) % 4, i) for i in range(4)])  4.77 us
    pallas_call x1, Pallas kernels, local(): pl.pallas_call(prep_kernel, out_shape=[pltpu.VMEM((rows, cols), BF), pltp...  4.46 us
    pallas_call x1, Pallas kernels, local(): pl.pallas_call(pick_kernel, out_shape=[pltpu.VMEM((halo, full), BF)] + [p...  2.89 us
    ppermute x1, starting transfers between devices, local(): lax.ppermute(other, 'dom', swap)  2.53 us
    pallas_call x1, Pallas kernels, local(): pl.pallas_call(own_kernel, out_shape=[pltpu.VMEM((rows, full), F32), pltp...  2.45 us
  transfers between devices with their start and end apart: 11, of which 4 were waited for; matrix products, arithmetic and copies ran while one was open for 0% of the time, Pallas kernels for 13%

profile of v2, /device:TPU:1, one launch (start us, length us, event | category | flops | bytes accessed | tf_op | source)
XLA Modules:
  0.0 53.6 jit_solution(17492799848746137071)
XLA Ops:
  0.0 2.9 %pick.1 = (bf16[512,256]{1,0:T(8,128)(2,1)}, bf16[352,256]{1,0:T(8,128)(2,1)S(1)}, bf16[352,256]{1,0:T(8,128)(2,1)S(1)}) custom-call(s32[8,64]{1,0:T(8,128)} %bitcast.11, bf16[64,2048]{1,0:T(8,128)(2,1)} %bitcast.10, bf16[2,64,2048]{2,1,0:T(8,128)(2,1)} %bitcast.9, bf16[3,64,256]{2,1,0:T(8,128)(2,1)} %weight_hbm.1), custom_call_target="tpu_custom_call" | custom-call | tf_op jit(solution)/shard_map/pick/pallas_call | solution.py:205
  2.9 11.9 %all-to-all-start = ((bf16[32,16,256]{2,1,0:T(8,128)(2,1)}), bf16[32,16,256]{2,1,0:T(8,128)(2,1)S(1)}, u32[]{:S(2)}, u32[]{:S(2)}) async-start(bf16[32,16,256]{2,1,0:T(8,128)(2,1)} %bitcast.5), calls=%async_computation | async-start | bytes 524288 | tf_op jit(solution)/shard_map/all_to_all | solution.py:228
  14.8 2.8 %collective-permute-start.1 = (bf16[352,256]{1,0:T(8,128)(2,1)S(1)}, bf16[352,256]{1,0:T(8,128)(2,1)S(1)}, u32[]{:S(2)}, u32[]{:S(2)}) collective-permute-start(bf16[352,256]{1,0:T(8,128)(2,1)S(1)} %get-tuple-element.18.a0), channel_id=1, source_target_pairs={{1,0},{2,1},{3,2},{0,3},{5,4},{6,5},{7,6},{4,7},{9,8},{10,9},{11,1... | collective-permute-start | bytes 540680 | tf_op jit(solution)/shard_map/ppermute | solution.py:186
  17.6 0.0 collective-permute-start.3
  17.6 0.0 collective-permute-start.5
  17.6 2.7 %collective-permute-start.6 = (bf16[352,256]{1,0:T(8,128)(2,1)S(1)}, bf16[352,256]{1,0:T(8,128)(2,1)S(1)}, u32[]{:S(2)}, u32[]{:S(2)}) collective-permute-start(bf16[352,256]{1,0:T(8,128)(2,1)S(1)} %get-tuple-element.19.b0), channel_id=1, source_target_pairs={{1,0},{2,1},{3,2},{0,3},{5,4},{6,5},{7,6},{4,7},{9,8},{10,9},{11,1... | collective-permute-start | bytes 540680 | tf_op jit(solution)/shard_map/ppermute | solution.py:186
  20.3 0.2 collective-permute-done.1.a1
  20.5 3.4 %collective-permute-start.2 = (bf16[352,256]{1,0:T(8,128)(2,1)S(1)}, bf16[352,256]{1,0:T(8,128)(2,1)S(1)}, u32[]{:S(2)}, u32[]{:S(2)}) collective-permute-start(bf16[352,256]{1,0:T(8,128)(2,1)S(1)} %collective-permute-done.1.a1), channel_id=1, source_target_pairs={{1,0},{2,1},{3,2},{0,3},{5,4},{6,5},{7,6},{4,7},{9,8},{10,9},{11,1... | collective-permute-start | bytes 540680 | tf_op jit(solution)/shard_map/ppermute | solution.py:186
  23.9 0.0 collective-permute-done.3.b3
  23.9 0.0 collective-permute-start.4
  23.9 2.1 %all-to-all-done.got_ref = bf16[32,16,256]{2,1,0:T(8,128)(2,1)S(1)} async-done(((bf16[32,16,256]{2,1,0:T(8,128)(2,1)}), bf16[32,16,256]{2,1,0:T(8,128)(2,1)S(1)}, u32[]{:S(2)}, u32[]{:S(2)}) %all-to-all-start) | async-done | bytes 262176 | tf_op jit(solution)/shard_map/all_to_all | solution.py:228
  26.0 2.5 %collective-permute-start = (bf16[256,256]{1,0:T(8,128)(2,1)S(1)}, bf16[256,256]{1,0:T(8,128)(2,1)S(1)}, u32[]{:S(2)}, u32[]{:S(2)}) collective-permute-start(bf16[256,256]{1,0:T(8,128)(2,1)S(1)} %get-tuple-element.17), channel_id=1, source_target_pairs={{0,4},{4,0},{8,12},{12,8},{16,20},{20,16},{24,28},{28,24},{32,36},... | collective-permute-start | bytes 393224 | tf_op jit(solution)/shard_map/ppermute | solution.py:247
  28.5 1.0 %collective-permute-done.other_ref = bf16[256,256]{1,0:T(8,128)(2,1)S(1)} collective-permute-done((bf16[256,256]{1,0:T(8,128)(2,1)S(1)}, bf16[256,256]{1,0:T(8,128)(2,1)S(1)}, u32[]{:S(2)}, u32[]{:S(2)}) %collective-permute-start) | collective-permute-done | bytes 131104 | tf_op jit(solution)/shard_map/ppermute | solution.py:247
  29.5 0.1 merge.1._.b0
  29.6 2.8 %collective-permute-start.7 = (bf16[768,128]{1,0:T(8,128)(2,1)S(1)}, bf16[768,128]{1,0:T(8,128)(2,1)S(1)}, u32[]{:S(2)}, u32[]{:S(2)}) collective-permute-start(bf16[768,128]{1,0:T(8,128)(2,1)S(1)} %merge.1._.b0), channel_id=1, source_target_pairs={{1,0},{2,1},{3,2},{0,3},{5,4},{6,5},{7,6},{4,7},{9,8},{10,9},{11,1... | collective-permute-start | bytes 589832 | tf_op jit(solution)/shard_map/ppermute | solution.py:186
  32.4 0.0 collective-permute-done.5._a.a3
  32.4 0.3 collective-permute-start.8
  32.8 0.0 collective-permute-done.6._b.b1
  32.8 0.7 %collective-permute-start.9 = (bf16[768,128]{1,0:T(8,128)(2,1)S(1)}, bf16[768,128]{1,0:T(8,128)(2,1)S(1)}, u32[]{:S(2)}, u32[]{:S(2)}) collective-permute-start(bf16[768,128]{1,0:T(8,128)(2,1)S(1)} %merge.1._.b0), channel_id=1, source_target_pairs={{3,0},{0,1},{1,2},{2,3},{7,4},{4,5},{5,6},{6,7},{11,8},{8,9},{9,10... | collective-permute-start | bytes 589832 | tf_op jit(solution)/shard_map/ppermute | solution.py:186
  33.5 0.0 collective-permute-done.2.__.a2
  33.5 0.0 collective-permute-done.4.___.b2
  33.5 4.5 %prep.1 = (bf16[2048,2560]{1,0:T(8,128)(2,1)S(1)}, f32[2048,128]{1,0:T(8,128)S(1)}) custom-call(s32[16,20]{1,0:T(8,128)} %mask_hbm.1, bf16[2048,2560]{1,0:T(8,128)(2,1)} %adj_hbm.1, bf16[768,128]{1,0:T(8,128)(2,1)S(1)} %merge.1._.b0, bf16[352,256]{1,0:T(8,128)(2,1)S(1)} %collective-permute-done.2.__.a2, bf16[352,256]{1,0:T(8,128)(2,1)S(1)} %collective-permute-done.4.___.b2, ...), custom_call_target="tpu_custom_call" | custom-call | flops 4300000256 | bytes 1000 | tf_op jit(solution)/shard_map/prep/pallas_call | solution.py:250
  38.0 2.4 %own.1 = (f32[2048,256]{1,0:T(8,128)S(1)}, f32[2048,256]{1,0:T(8,128)S(1)}, bf16[3,256,256]{2,1,0:T(8,128)(2,1)S(1)}) custom-call(s32[1]{0:T(128)} %bitcast.6.place_ref, bf16[2048,2560]{1,0:T(8,128)(2,1)S(1)} %get-tuple-element.20.masked_ref, bf16[352,256]{1,0:T(8,128)(2,1)S(1)} %get-tuple-element.18.a0, bf16[352,256]{1,0:T(8,128)(2,1)S(1)} %collective-permute-done.1.a1, ...), custom_call_target="tpu_custom_call" | custom-call | flops 1000 | bytes 1000 | tf_op jit(solution)/shard_map/own/pallas_call | solution.py:261
  40.4 0.0 collective-permute-done.7.b1
  40.4 0.0 collective-permute-done.8.b2
  40.4 4.5 %collective-permute-done.9.b3 = bf16[768,128]{1,0:T(8,128)(2,1)S(1)} collective-permute-done((bf16[768,128]{1,0:T(8,128)(2,1)S(1)}, bf16[768,128]{1,0:T(8,128)(2,1)S(1)}, u32[]{:S(2)}, u32[]{:S(2)}) %collective-permute-start.9) | collective-permute-done | bytes 196640 | tf_op jit(solution)/shard_map/ppermute | solution.py:186
  45.0 8.7 %tail.1 = bf16[64,2048]{1,0:T(8,128)(2,1)} custom-call(bf16[2048,2560]{1,0:T(8,128)(2,1)S(1)} %get-tuple-element.20.masked_ref, f32[2048,128]{1,0:T(8,128)S(1)} %get-tuple-element.21.scale_ref, f32[2048,256]{1,0:T(8,128)S(1)} %get-tuple-element.22.sums_ref, f32[2048,256]{1,0:T(8,128)S(1)} %get-tuple-element.23.rest_ref, ...), custom_call_target="tpu_custom_call" | custom-call | tf_op jit(solution)/shard_map/tail/pallas_call | solution.py:276
  (1 shorter events, 0.0 us)
Async XLA Ops:
  2.9 23.1 %all-to-all-start = ((bf16[32,16,256]{2,1,0:T(8,128)(2,1)}), bf16[32,16,256]{2,1,0:T(8,128)(2,1)S(1)}, u32[]{:S(2)}, u32[]{:S(2)}) async-start(bf16[32,16,256]{2,1,0:T(8,128)(2,1)} %bitcast.5), calls=%async_computation | async-start | bytes 524288 | tf_op jit(solution)/shard_map/all_to_all | solution.py:228
  14.8 5.7 %collective-permute-start.1 = (bf16[352,256]{1,0:T(8,128)(2,1)S(1)}, bf16[352,256]{1,0:T(8,128)(2,1)S(1)}, u32[]{:S(2)}, u32[]{:S(2)}) collective-permute-start(bf16[352,256]{1,0:T(8,128)(2,1)S(1)} %get-tuple-element.18.a0), channel_id=1, source_target_pairs={{1,0},{2,1},{3,2},{0,3},{5,4},{6,5},{7,6},{4,7},{9,8},{10,9},{11,1... | collective-permute-start | bytes 540680 | tf_op jit(solution)/shard_map/ppermute | solution.py:186
  17.6 6.3 %collective-permute-start.3 = (bf16[352,256]{1,0:T(8,128)(2,1)S(1)}, bf16[352,256]{1,0:T(8,128)(2,1)S(1)}, u32[]{:S(2)}, u32[]{:S(2)}) collective-permute-start(bf16[352,256]{1,0:T(8,128)(2,1)S(1)} %get-tuple-element.19.b0), channel_id=1, source_target_pairs={{3,0},{0,1},{1,2},{2,3},{7,4},{4,5},{5,6},{6,7},{11,8},{8,9},{9,10... | collective-permute-start | bytes 540680 | tf_op jit(solution)/shard_map/ppermute | solution.py:186
  17.6 14.8 %collective-permute-start.5 = (bf16[352,256]{1,0:T(8,128)(2,1)S(1)}, bf16[352,256]{1,0:T(8,128)(2,1)S(1)}, u32[]{:S(2)}, u32[]{:S(2)}) collective-permute-start(bf16[352,256]{1,0:T(8,128)(2,1)S(1)} %get-tuple-element.18.a0), channel_id=1, source_target_pairs={{3,0},{0,1},{1,2},{2,3},{7,4},{4,5},{5,6},{6,7},{11,8},{8,9},{9,10... | collective-permute-start | bytes 540680 | tf_op jit(solution)/shard_map/ppermute | solution.py:186
  17.6 15.2 %collective-permute-start.6 = (bf16[352,256]{1,0:T(8,128)(2,1)S(1)}, bf16[352,256]{1,0:T(8,128)(2,1)S(1)}, u32[]{:S(2)}, u32[]{:S(2)}) collective-permute-start(bf16[352,256]{1,0:T(8,128)(2,1)S(1)} %get-tuple-element.19.b0), channel_id=1, source_target_pairs={{1,0},{2,1},{3,2},{0,3},{5,4},{6,5},{7,6},{4,7},{9,8},{10,9},{11,1... | collective-permute-start | bytes 540680 | tf_op jit(solution)/shard_map/ppermute | solution.py:186
  20.5 13.0 %collective-permute-start.2 = (bf16[352,256]{1,0:T(8,128)(2,1)S(1)}, bf16[352,256]{1,0:T(8,128)(2,1)S(1)}, u32[]{:S(2)}, u32[]{:S(2)}) collective-permute-start(bf16[352,256]{1,0:T(8,128)(2,1)S(1)} %collective-permute-done.1.a1), channel_id=1, source_target_pairs={{1,0},{2,1},{3,2},{0,3},{5,4},{6,5},{7,6},{4,7},{9,8},{10,9},{11,1... | collective-permute-start | bytes 540680 | tf_op jit(solution)/shard_map/ppermute | solution.py:186
  23.9 9.6 %collective-permute-start.4 = (bf16[352,256]{1,0:T(8,128)(2,1)S(1)}, bf16[352,256]{1,0:T(8,128)(2,1)S(1)}, u32[]{:S(2)}, u32[]{:S(2)}) collective-permute-start(bf16[352,256]{1,0:T(8,128)(2,1)S(1)} %collective-permute-done.3.b3), channel_id=1, source_target_pairs={{3,0},{0,1},{1,2},{2,3},{7,4},{4,5},{5,6},{6,7},{11,8},{8,9},{9,10... | collective-permute-start | bytes 540680 | tf_op jit(solution)/shard_map/ppermute | solution.py:186
  26.0 3.5 %collective-permute-start = (bf16[256,256]{1,0:T(8,128)(2,1)S(1)}, bf16[256,256]{1,0:T(8,128)(2,1)S(1)}, u32[]{:S(2)}, u32[]{:S(2)}) collective-permute-start(bf16[256,256]{1,0:T(8,128)(2,1)S(1)} %get-tuple-element.17), channel_id=1, source_target_pairs={{0,4},{4,0},{8,12},{12,8},{16,20},{20,16},{24,28},{28,24},{32,36},... | collective-permute-start | bytes 393224 | tf_op jit(solution)/shard_map/ppermute | solution.py:247
  29.6 10.8 %collective-permute-start.7 = (bf16[768,128]{1,0:T(8,128)(2,1)S(1)}, bf16[768,128]{1,0:T(8,128)(2,1)S(1)}, u32[]{:S(2)}, u32[]{:S(2)}) collective-permute-start(bf16[768,128]{1,0:T(8,128)(2,1)S(1)} %merge.1._.b0), channel_id=1, source_target_pairs={{1,0},{2,1},{3,2},{0,3},{5,4},{6,5},{7,6},{4,7},{9,8},{10,9},{11,1... | collective-permute-start | bytes 589832 | tf_op jit(solution)/shard_map/ppermute | solution.py:186
  32.4 8.0 %collective-permute-start.8 = (bf16[768,128]{1,0:T(8,128)(2,1)S(1)}, bf16[768,128]{1,0:T(8,128)(2,1)S(1)}, u32[]{:S(2)}, u32[]{:S(2)}) collective-permute-start(bf16[768,128]{1,0:T(8,128)(2,1)S(1)} %merge.1._.b0), channel_id=1, source_target_pairs={{2,0},{3,1},{0,2},{1,3},{6,4},{7,5},{4,6},{5,7},{10,8},{11,9},{8,1... | collective-permute-start | bytes 589832 | tf_op jit(solution)/shard_map/ppermute | solution.py:186
  32.8 12.2 %collective-permute-start.9 = (bf16[768,128]{1,0:T(8,128)(2,1)S(1)}, bf16[768,128]{1,0:T(8,128)(2,1)S(1)}, u32[]{:S(2)}, u32[]{:S(2)}) collective-permute-start(bf16[768,128]{1,0:T(8,128)(2,1)S(1)} %merge.1._.b0), channel_id=1, source_target_pairs={{3,0},{0,1},{1,2},{2,3},{7,4},{4,5},{5,6},{6,7},{11,8},{8,9},{9,10... | collective-permute-start | bytes 589832 | tf_op jit(solution)/shard_map/ppermute | solution.py:186

commit v3 on v2

--- a/solution.py
+++ b/solution.py
@@ -64,50 +64,26 @@
     out_ref[:, : layers * width] = nt_dot(chosen_ref[...], source_ref[...]).astype(BF)
 
 
-def split_kernel(core_ref, got_ref, mine_ref, other_ref):
-    chips = got_ref.shape[0]
-    full = got_ref.shape[2]
-    low, high = got_ref[:, :8, :], got_ref[:, 8:, :]
-    first = core_ref[0] == 0
-    mine_ref[...] = jnp.where(first, low, high).reshape(chips * 8, full)
-    other_ref[...] = jnp.where(first, high, low).reshape(chips * 8, full)
-
-
-def merge_kernel(core_ref, mine_ref, other_ref, out_ref):
-    count, full = mine_ref.shape
-    chips = count // 8
-    halo = 2 * count
-    first = core_ref[0] == 0
-    mine = mine_ref[...].reshape(chips, 8, full)
-    other = other_ref[...].reshape(chips, 8, full)
-    low, high = jnp.where(first, mine, other), jnp.where(first, other, mine)
-    got = jnp.concatenate([low, high], axis=1).reshape(halo, full)
-    out_ref[:halo, :] = got[:, :128]
-    out_ref[halo:, :64] = got[:count, 128:192]
-    out_ref[halo:, 64:] = got[count:, 128:192]
-
-
-def prep_kernel(mask_hbm, adj_hbm, _, __, ___, _a, _b, masked_ref, scale_ref, mask_ref, sems):
+def compact_kernel(got_ref, near_ref, far_ref, whole_ref):
+    halo = got_ref.shape[0]
+    half = halo // 2
+    near_ref[:, :64] = got_ref[:half, :64]
+    near_ref[:, 64:] = got_ref[half:, :64]
+    far = got_ref[:, 64:192]
+    far_ref[...] = far
+    whole_ref[:half, :64] = got_ref[:half, :64]
+    whole_ref[:half, 64:] = got_ref[half:, :64]
+    whole_ref[half:, :] = far
+
+
+def prep_kernel(mask_ref, adj_ref, _, __, ___, _a, _b, masked_ref, scale_ref):
     rows, cols = masked_ref.shape
-    chunk = rows // (sems.shape[0] - 1)
-    mask_copy = pltpu.make_async_copy(mask_hbm, mask_ref, sems.at[rows // chunk])
-    mask_copy.start()
-
-    def copy(i):
-        part = pl.ds(i * chunk, chunk)
-        return pltpu.make_async_copy(adj_hbm.at[part, :], masked_ref.at[part, :], sems.at[i])
-
-    for i in range(rows // chunk):
-        copy(i).start()
-    mask_copy.wait()
     for i in range(rows // TILE):
-        if i * TILE % chunk == 0:
-            copy(i * TILE // chunk).wait()
         part = pl.ds(i * TILE, TILE)
         total = jnp.zeros((TILE, TILE), F32)
         for t in range(cols // TILE):
             keep = mask_ref[i, t].astype(F32).astype(BF)
-            tile = masked_ref[part, t * TILE : (t + 1) * TILE] * keep
+            tile = adj_ref[part, t * TILE : (t + 1) * TILE] * keep
             masked_ref[part, t * TILE : (t + 1) * TILE] = tile
             total += tile.astype(F32)
         scale = 0.9 / (1.0 + jnp.sum(total, axis=1, keepdims=True))
@@ -160,26 +136,39 @@
             made_ref[part, :] = made
 
 
-def tail_kernel(masked_ref, scale_ref, sums_ref, rest_ref, weight_ref, b0, b1, b2, b3, out_ref, first, second, acc_ref):
+def early_kernel(masked_ref, scale_ref, sums_ref, rest_ref, weight_ref, b0, b1, b2, b3, next_ref, border, made, acc_ref):
     rows, cols = masked_ref.shape
-    halo = cols - rows
-    half = halo // 2
-    packs = (b0, b1, b2, b3)
+    half = b2.shape[0]
+    packs = [pack[:half, :] for pack in (b0, b1, b2, b3)]
     block = 1024
-    border = jnp.concatenate([pack[:halo, :64] for pack in packs], axis=1)
-    first[rows:, :] = jnp.concatenate([pack[:halo, 64:] for pack in packs], axis=1)
-    second[rows : rows + half, :] = jnp.concatenate([pack[halo:, :64] for pack in packs], axis=1)
-    second[rows + half :, :] = jnp.concatenate([pack[halo:, 64:] for pack in packs], axis=1)
+    border[:half, :] = jnp.concatenate([pack[:, :64] for pack in packs], axis=1)
+    border[half:, :] = jnp.concatenate([pack[:, 64:] for pack in packs], axis=1)
+    for begin in range(0, rows, block):
+        whole = pl.ds(begin, block)
+        more = jnp.dot(masked_ref[whole, rows:], border[...], preferred_element_type=F32)
+        acc_ref[whole, :] = sums_ref[whole, :] + more
+    finish(0, acc_ref, scale_ref, rest_ref, weight_ref, made)
+    for begin in range(0, rows, block):
+        whole = pl.ds(begin, block)
+        next_ref[whole, :] = jnp.dot(masked_ref[whole, :rows], made[...], preferred_element_type=F32)
+
+
+def late_kernel(masked_ref, scale_ref, sums_ref, rest_ref, weight_ref, b0, b1, b2, b3, out_ref, joined, acc_ref):
+    rows, cols = masked_ref.shape
+    half = (cols - rows) // 2
+    packs = (b0[half:, :], b1[half:, :], b2[...], b3[half:, :])
+    block = 1024
+    border = jnp.concatenate([pack[:, :64] for pack in packs], axis=1)
+    joined[rows:, :] = jnp.concatenate([pack[:, 64:] for pack in packs], axis=1)
     for begin in range(0, rows, block):
         whole = pl.ds(begin, block)
         more = jnp.dot(masked_ref[whole, rows:], border, preferred_element_type=F32)
         acc_ref[whole, :] = sums_ref[whole, :] + more
-    finish(0, acc_ref, scale_ref, rest_ref, weight_ref, first)
-    for depth, joined, made_ref in ((1, first, second), (2, second, out_ref)):
-        for begin in range(0, rows, block):
-            whole = pl.ds(begin, block)
-            acc_ref[whole, :] = jnp.dot(masked_ref[whole, :], joined[...], preferred_element_type=F32)
-        finish(depth, acc_ref, scale_ref, rest_ref, weight_ref, made_ref)
+    finish(1, acc_ref, scale_ref, rest_ref, weight_ref, joined)
+    for begin in range(0, rows, block):
+        whole = pl.ds(begin, block)
+        acc_ref[whole, :] = jnp.dot(masked_ref[whole, :], joined[...], preferred_element_type=F32)
+    finish(2, acc_ref, scale_ref, rest_ref, weight_ref, out_ref)
 
 
 def ring(x, shift):
@@ -221,42 +210,29 @@
     b1, b3 = ring(pack_b, 1), ring(pack_b, 3)
     packs = [pack_a, a1, ring(a1, 1), a3, pack_b, b1, ring(b3, 3), b3]
 
-    cores = 2
-    chips = peers // cores
-    core = lax.rem(lax.axis_index("dom"), cores).astype(jnp.int32).reshape(1)
-    groups = [[chip * cores + c for chip in range(chips)] for c in range(cores)]
-    arrived = lax.all_to_all(
-        outgoing.reshape(chips, cores * slots, full), "dom", split_axis=0, concat_axis=0, tiled=True, axis_index_groups=groups
-    )
-    mine, other = pl.pallas_call(
-        split_kernel,
-        out_shape=[pltpu.VMEM((halo // 2, full), BF)] * 2,
-        in_specs=[smem, vmem],
-        out_specs=[vmem] * 2,
-        compiler_params=params(vmem_limit_bytes=4 * MIB),
-        name="split",
-    )(core, in_vmem(arrived))
-    swap = [(i, i ^ 1) for i in range(peers)]
-    border = pl.pallas_call(
-        merge_kernel,
-        out_shape=pltpu.VMEM((halo + halo // 2, 128), BF),
-        in_specs=[smem, vmem, vmem],
-        out_specs=vmem,
-        compiler_params=params(vmem_limit_bytes=4 * MIB),
-        name="merge",
-    )(core, in_vmem(mine), in_vmem(lax.ppermute(other, "dom", swap)))
-    borders = [border] + [ring(border, shift) for shift in (1, 2, 3)]
+    arrived = lax.all_to_all(outgoing.reshape(peers, slots, full), "dom", split_axis=0, concat_axis=0, tiled=True)
+    near, far, whole = pl.pallas_call(
+        compact_kernel,
+        out_shape=[pltpu.VMEM((size, 128), BF) for size in (halo // 2, halo, halo + halo // 2)],
+        in_specs=[vmem],
+        out_specs=[vmem] * 3,
+        compiler_params=params(vmem_limit_bytes=2 * MIB),
+        cost_estimate=pl.CostEstimate(flops=15000000000, bytes_accessed=1000, transcendentals=0),
+        name="compact",
+    )(in_vmem(arrived.reshape(halo, full)))
+    after_all, before_all = ring(whole, 1), ring(whole, 3)
+    nears = [whole, after_all, ring(near, 2), before_all]
+    fars = [whole, after_all, ring(far, 2), before_all]
 
     masked, scale = pl.pallas_call(
         prep_kernel,
         out_shape=[pltpu.VMEM((rows, cols), BF), pltpu.VMEM((rows, 128), F32)],
-        in_specs=[hbm, hbm] + [vmem] * 5,
+        in_specs=[smem] + [vmem] * 6,
         out_specs=[vmem] * 2,
-        scratch_shapes=[pltpu.SMEM(tile_mask.shape, jnp.int32), pltpu.SemaphoreType.DMA((9,))],
-        compiler_params=params(vmem_limit_bytes=4 * MIB),
-        cost_estimate=pl.CostEstimate(flops=4_300_000_000, bytes_accessed=1000, transcendentals=0),
+        compiler_params=params(vmem_limit_bytes=14 * MIB),
+        cost_estimate=pl.CostEstimate(flops=4300001000, bytes_accessed=1000, transcendentals=0),
         name="prep",
-    )(in_hbm(tile_mask), in_hbm(adjacency), in_vmem(border), *[in_vmem(packs[k]) for k in (2, 6, 3, 5)])
+    )(tile_mask, adjacency, in_vmem(near), *[in_vmem(packs[k]) for k in (2, 6, 3, 5)])
 
     sums, rest, turned = pl.pallas_call(
         own_kernel,
@@ -269,19 +245,30 @@
         out_specs=[vmem] * 3,
         scratch_shapes=[pltpu.VMEM((rows, full), BF)],
         compiler_params=params(vmem_limit_bytes=8 * MIB),
-        cost_estimate=pl.CostEstimate(flops=1000, bytes_accessed=1000, transcendentals=0),
+        cost_estimate=pl.CostEstimate(flops=2100001000, bytes_accessed=1000, transcendentals=0),
         name="own",
     )(place, in_vmem(masked), *[in_vmem(p) for p in packs])
 
+    sums = pl.pallas_call(
+        early_kernel,
+        out_shape=pltpu.VMEM((rows, full), F32),
+        in_specs=[vmem] * 9,
+        out_specs=vmem,
+        scratch_shapes=[pltpu.VMEM((halo, full), BF), pltpu.VMEM((rows, full), BF), pltpu.VMEM((rows, full), F32)],
+        compiler_params=params(vmem_limit_bytes=10 * MIB),
+        cost_estimate=pl.CostEstimate(flops=1000, bytes_accessed=1000, transcendentals=0),
+        name="early",
+    )(*[in_vmem(x) for x in (masked, scale, sums, rest, turned, *nears)])
+
     out = pl.pallas_call(
-        tail_kernel,
+        late_kernel,
         out_shape=jax.ShapeDtypeStruct((width, rows), BF),
         in_specs=[vmem] * 9,
         out_specs=vmem,
-        scratch_shapes=[pltpu.VMEM((cols, full), BF), pltpu.VMEM((cols, full), BF), pltpu.VMEM((rows, full), F32)],
-        compiler_params=params(vmem_limit_bytes=12 * MIB),
-        name="tail",
-    )(*[in_vmem(x) for x in (masked, scale, sums, rest, turned, *borders)])
+        scratch_shapes=[pltpu.VMEM((cols, full), BF), pltpu.VMEM((rows, full), F32)],
+        compiler_params=params(vmem_limit_bytes=10 * MIB),
+        name="late",
+    )(*[in_vmem(x) for x in (masked, scale, sums, rest, turned, *fars)])
     return out.T
 
 

time: 53.9 us -> 50.6 us (0.939)
  the two profiles are of different devices: /device:TPU:1 before, /device:TPU:2 now
where the time goes in v3:
time: 50.6 us; the launch traced here: 50.4 us
  starting transfers between devices  27.9 us (55%)
  Pallas kernels  17.1 us (34%)
  waiting for transfers between devices  5.43 us (11%)
    ppermute x10, starting transfers between devices, ring(): return lax.ppermute(x, 'feat', [((i + shift) % 4, i) for i in range(4)])  15.8 us
    all_to_all x1, starting transfers between devices, local(): lax.all_to_all(outgoing.reshape(peers, slots, full), 'dom', split_axis=0,...  12 us
    pallas_call x1, Pallas kernels, local(): pl.pallas_call(late_kernel, out_shape=jax.ShapeDtypeStruct((width, rows),...  5.15 us
    ppermute x10, waiting for transfers between devices, ring(): return lax.ppermute(x, 'feat', [((i + shift) % 4, i) for i in range(4)])  4.95 us
    pallas_call x1, Pallas kernels, local(): pl.pallas_call(early_kernel, out_shape=pltpu.VMEM((rows, full), F32), in_...  3.45 us
    pallas_call x1, Pallas kernels, local(): pl.pallas_call(prep_kernel, out_shape=[pltpu.VMEM((rows, cols), BF), pltp...  2.92 us
    pallas_call x1, Pallas kernels, local(): pl.pallas_call(pick_kernel, out_shape=[pltpu.VMEM((halo, full), BF)] + [p...  2.89 us
    pallas_call x1, Pallas kernels, local(): pl.pallas_call(own_kernel, out_shape=[pltpu.VMEM((rows, full), F32), pltp...  2.45 us
  transfers between devices with their start and end apart: 11, of which 5 were waited for; matrix products, arithmetic and copies ran while one was open for 0% of the time, Pallas kernels for 18%

profile of v3, /device:TPU:2, one launch (start us, length us, event | category | flops | bytes accessed | tf_op | source)
XLA Modules:
  0.0 50.4 jit_solution(9034315825030020846)
XLA Ops:
  0.0 2.9 %pick.1 = (bf16[512,256]{1,0:T(8,128)(2,1)}, bf16[352,256]{1,0:T(8,128)(2,1)S(1)}, bf16[352,256]{1,0:T(8,128)(2,1)S(1)}) custom-call(s32[8,64]{1,0:T(8,128)} %bitcast.12, bf16[64,2048]{1,0:T(8,128)(2,1)} %bitcast.11, bf16[2,64,2048]{2,1,0:T(8,128)(2,1)} %bitcast.10, bf16[3,64,256]{2,1,0:T(8,128)(2,1)} %weight_hbm.1), custom_call_target="tpu_custom_call" | custom-call | tf_op jit(solution)/shard_map/pick/pallas_call | solution.py:194
  2.9 12.0 %all-to-all-start = ((bf16[64,8,256]{2,1,0:T(8,128)(2,1)}), bf16[64,8,256]{2,1,0:T(8,128)(2,1)S(1)}, u32[]{:S(2)}, u32[]{:S(2)}) async-start(bf16[64,8,256]{2,1,0:T(8,128)(2,1)} %bitcast.4), calls=%async_computation | async-start | bytes 524288 | tf_op jit(solution)/shard_map/all_to_all | solution.py:213
  14.9 3.1 %collective-permute-start = (bf16[352,256]{1,0:T(8,128)(2,1)S(1)}, bf16[352,256]{1,0:T(8,128)(2,1)S(1)}, u32[]{:S(2)}, u32[]{:S(2)}) collective-permute-start(bf16[352,256]{1,0:T(8,128)(2,1)S(1)} %get-tuple-element.18.a0), channel_id=1, source_target_pairs={{1,0},{2,1},{3,2},{0,3},{5,4},{6,5},{7,6},{4,7},{9,8},{10,9},{11,1... | collective-permute-start | bytes 540680 | tf_op jit(solution)/shard_map/ppermute | solution.py:175
  18.0 0.0 collective-permute-start.2
  18.0 0.6 %collective-permute-start.4 = (bf16[352,256]{1,0:T(8,128)(2,1)S(1)}, bf16[352,256]{1,0:T(8,128)(2,1)S(1)}, u32[]{:S(2)}, u32[]{:S(2)}) collective-permute-start(bf16[352,256]{1,0:T(8,128)(2,1)S(1)} %get-tuple-element.18.a0), channel_id=1, source_target_pairs={{3,0},{0,1},{1,2},{2,3},{7,4},{4,5},{5,6},{6,7},{11,8},{8,9},{9,10... | collective-permute-start | bytes 540680 | tf_op jit(solution)/shard_map/ppermute | solution.py:175
  18.6 2.7 %collective-permute-start.5 = (bf16[352,256]{1,0:T(8,128)(2,1)S(1)}, bf16[352,256]{1,0:T(8,128)(2,1)S(1)}, u32[]{:S(2)}, u32[]{:S(2)}) collective-permute-start(bf16[352,256]{1,0:T(8,128)(2,1)S(1)} %get-tuple-element.19.b0), channel_id=1, source_target_pairs={{1,0},{2,1},{3,2},{0,3},{5,4},{6,5},{7,6},{4,7},{9,8},{10,9},{11,1... | collective-permute-start | bytes 540680 | tf_op jit(solution)/shard_map/ppermute | solution.py:175
  21.3 1.6 %collective-permute-done.a1 = bf16[352,256]{1,0:T(8,128)(2,1)S(1)} collective-permute-done((bf16[352,256]{1,0:T(8,128)(2,1)S(1)}, bf16[352,256]{1,0:T(8,128)(2,1)S(1)}, u32[]{:S(2)}, u32[]{:S(2)}) %collective-permute-start) | collective-permute-done | bytes 180256 | tf_op jit(solution)/shard_map/ppermute | solution.py:175
  22.9 3.7 %collective-permute-start.1 = (bf16[352,256]{1,0:T(8,128)(2,1)S(1)}, bf16[352,256]{1,0:T(8,128)(2,1)S(1)}, u32[]{:S(2)}, u32[]{:S(2)}) collective-permute-start(bf16[352,256]{1,0:T(8,128)(2,1)S(1)} %collective-permute-done.a1), channel_id=1, source_target_pairs={{1,0},{2,1},{3,2},{0,3},{5,4},{6,5},{7,6},{4,7},{9,8},{10,9},{11,1... | collective-permute-start | bytes 540680 | tf_op jit(solution)/shard_map/ppermute | solution.py:175
  26.6 0.0 collective-permute-done.2.b3
  26.7 0.0 collective-permute-start.3
  26.7 0.5 all-to-all-done
  27.2 0.0 copy-start
  27.2 0.0 copy-start.1
  27.2 0.2 compact.1
  27.4 1.6 %collective-permute-start.8 = (bf16[768,128]{1,0:T(8,128)(2,1)S(1)}, bf16[768,128]{1,0:T(8,128)(2,1)S(1)}, u32[]{:S(2)}, u32[]{:S(2)}) collective-permute-start(bf16[768,128]{1,0:T(8,128)(2,1)S(1)} %get-tuple-element.25.b0), channel_id=1, source_target_pairs={{3,0},{0,1},{1,2},{2,3},{7,4},{4,5},{5,6},{6,7},{11,8},{8,9},{9,10... | collective-permute-start | bytes 589832 | tf_op jit(solution)/shard_map/ppermute | solution.py:175
  29.0 1.1 %collective-permute-done.4._a.a3 = bf16[352,256]{1,0:T(8,128)(2,1)S(1)} collective-permute-done((bf16[352,256]{1,0:T(8,128)(2,1)S(1)}, bf16[352,256]{1,0:T(8,128)(2,1)S(1)}, u32[]{:S(2)}, u32[]{:S(2)}) %collective-permute-start.4) | collective-permute-done | bytes 180256 | tf_op jit(solution)/shard_map/ppermute | solution.py:175
  30.1 0.6 %collective-permute-start.6 = (bf16[768,128]{1,0:T(8,128)(2,1)S(1)}, bf16[768,128]{1,0:T(8,128)(2,1)S(1)}, u32[]{:S(2)}, u32[]{:S(2)}) collective-permute-start(bf16[768,128]{1,0:T(8,128)(2,1)S(1)} %get-tuple-element.25.b0), channel_id=1, source_target_pairs={{1,0},{2,1},{3,2},{0,3},{5,4},{6,5},{7,6},{4,7},{9,8},{10,9},{11,1... | collective-permute-start | bytes 589832 | tf_op jit(solution)/shard_map/ppermute | solution.py:175
  30.7 0.0 collective-permute-done.5._b.b1
  30.7 2.0 %collective-permute-start.7 = (bf16[256,128]{1,0:T(8,128)(2,1)S(1)}, bf16[256,128]{1,0:T(8,128)(2,1)S(1)}, u32[]{:S(2)}, u32[]{:S(2)}) collective-permute-start(bf16[256,128]{1,0:T(8,128)(2,1)S(1)} %get-tuple-element.17._), channel_id=1, source_target_pairs={{2,0},{3,1},{0,2},{1,3},{6,4},{7,5},{4,6},{5,7},{10,8},{11,9},{8,1... | collective-permute-start | bytes 196616 | tf_op jit(solution)/shard_map/ppermute | solution.py:175
  32.7 0.0 collective-permute-done.1.__.a2
  32.7 1.5 %collective-permute-start.9 = (bf16[512,128]{1,0:T(8,128)(2,1)S(1)}, bf16[512,128]{1,0:T(8,128)(2,1)S(1)}, u32[]{:S(2)}, u32[]{:S(2)}) collective-permute-start(bf16[512,128]{1,0:T(8,128)(2,1)S(1)} %get-tuple-element.26), channel_id=1, source_target_pairs={{2,0},{3,1},{0,2},{1,3},{6,4},{7,5},{4,6},{5,7},{10,8},{11,9},{8,1... | collective-permute-start | bytes 393224 | tf_op jit(solution)/shard_map/ppermute | solution.py:175
  34.2 1.1 %collective-permute-done.3.___.b2 = bf16[352,256]{1,0:T(8,128)(2,1)S(1)} collective-permute-done((bf16[352,256]{1,0:T(8,128)(2,1)S(1)}, bf16[352,256]{1,0:T(8,128)(2,1)S(1)}, u32[]{:S(2)}, u32[]{:S(2)}) %collective-permute-start.3) | collective-permute-done | bytes 180256 | tf_op jit(solution)/shard_map/ppermute | solution.py:175
  35.3 0.0 copy-done
  35.3 0.0 copy-done.1
  35.3 2.9 %prep.1 = (bf16[2048,2560]{1,0:T(8,128)(2,1)S(1)}, f32[2048,128]{1,0:T(8,128)S(1)}) custom-call(s32[16,20]{1,0:T(8,128)S(1)} %copy-done.1, bf16[2048,2560]{1,0:T(8,128)(2,1)S(1)} %copy-done, bf16[256,128]{1,0:T(8,128)(2,1)S(1)} %get-tuple-element.17._, bf16[352,256]{1,0:T(8,128)(2,1)S(1)} %collective-permute-done.1.__.a2, ...), custom_call_target="tpu_custom_call" | custom-call | flops 4300000768 | bytes 1000 | tf_op jit(solution)/shard_map/prep/pallas_call | solution.py:227
  38.2 2.5 %own.1 = (f32[2048,256]{1,0:T(8,128)S(1)}, f32[2048,256]{1,0:T(8,128)S(1)}, bf16[3,256,256]{2,1,0:T(8,128)(2,1)S(1)}) custom-call(s32[1]{0:T(128)} %bitcast.6.place_ref, bf16[2048,2560]{1,0:T(8,128)(2,1)S(1)} %get-tuple-element.20.masked_ref, bf16[352,256]{1,0:T(8,128)(2,1)S(1)} %get-tuple-element.18.a0, bf16[352,256]{1,0:T(8,128)(2,1)S(1)} %collective-permute-done.a1, ...), custom_call_target="tpu_custom_call" | custom-call | flops 2100001024 | bytes 1000 | tf_op jit(solution)/shard_map/own/pallas_call | solution.py:237
  40.7 0.0 collective-permute-done.7.b2
  40.7 1.1 %collective-permute-done.8.b3 = bf16[768,128]{1,0:T(8,128)(2,1)S(1)} collective-permute-done((bf16[768,128]{1,0:T(8,128)(2,1)S(1)}, bf16[768,128]{1,0:T(8,128)(2,1)S(1)}, u32[]{:S(2)}, u32[]{:S(2)}) %collective-permute-start.8) | collective-permute-done | bytes 196640 | tf_op jit(solution)/shard_map/ppermute | solution.py:175
  41.8 0.0 collective-permute-done.6.b1
  41.8 3.4 %early.1.sums_ref = f32[2048,256]{1,0:T(8,128)S(1)} custom-call(bf16[2048,2560]{1,0:T(8,128)(2,1)S(1)} %get-tuple-element.20.masked_ref, f32[2048,128]{1,0:T(8,128)S(1)} %get-tuple-element.21.scale_ref, f32[2048,256]{1,0:T(8,128)S(1)} %get-tuple-element.22.sums_ref, f32[2048,256]{1,0:T(8,128)S(1)} %get-tuple-element.23.rest_ref, ...), custom_call_target="tpu_custom_call" | custom-call | flops 1000 | bytes 1000 | tf_op jit(solution)/shard_map/early/pallas_call | solution.py:252
  45.2 0.0 collective-permute-done.9.b2
  45.3 5.1 %late.1 = bf16[64,2048]{1,0:T(8,128)(2,1)} custom-call(bf16[2048,2560]{1,0:T(8,128)(2,1)S(1)} %get-tuple-element.20.masked_ref, f32[2048,128]{1,0:T(8,128)S(1)} %get-tuple-element.21.scale_ref, f32[2048,256]{1,0:T(8,128)S(1)} %early.1.sums_ref, f32[2048,256]{1,0:T(8,128)S(1)} %get-tuple-element.23.rest_ref, ...), custom_call_target="tpu_custom_call" | custom-call | tf_op jit(solution)/shard_map/late/pallas_call | solution.py:263
Async XLA Ops:
  2.9 24.3 %all-to-all-start = ((bf16[64,8,256]{2,1,0:T(8,128)(2,1)}), bf16[64,8,256]{2,1,0:T(8,128)(2,1)S(1)}, u32[]{:S(2)}, u32[]{:S(2)}) async-start(bf16[64,8,256]{2,1,0:T(8,128)(2,1)} %bitcast.4), calls=%async_computation | async-start | bytes 524288 | tf_op jit(solution)/shard_map/all_to_all | solution.py:213
  14.9 8.0 %collective-permute-start = (bf16[352,256]{1,0:T(8,128)(2,1)S(1)}, bf16[352,256]{1,0:T(8,128)(2,1)S(1)}, u32[]{:S(2)}, u32[]{:S(2)}) collective-permute-start(bf16[352,256]{1,0:T(8,128)(2,1)S(1)} %get-tuple-element.18.a0), channel_id=1, source_target_pairs={{1,0},{2,1},{3,2},{0,3},{5,4},{6,5},{7,6},{4,7},{9,8},{10,9},{11,1... | collective-permute-start | bytes 540680 | tf_op jit(solution)/shard_map/ppermute | solution.py:175
  18.0 8.6 %collective-permute-start.2 = (bf16[352,256]{1,0:T(8,128)(2,1)S(1)}, bf16[352,256]{1,0:T(8,128)(2,1)S(1)}, u32[]{:S(2)}, u32[]{:S(2)}) collective-permute-start(bf16[352,256]{1,0:T(8,128)(2,1)S(1)} %get-tuple-element.19.b0), channel_id=1, source_target_pairs={{3,0},{0,1},{1,2},{2,3},{7,4},{4,5},{5,6},{6,7},{11,8},{8,9},{9,10... | collective-permute-start | bytes 540680 | tf_op jit(solution)/shard_map/ppermute | solution.py:175
  18.0 12.1 %collective-permute-start.4 = (bf16[352,256]{1,0:T(8,128)(2,1)S(1)}, bf16[352,256]{1,0:T(8,128)(2,1)S(1)}, u32[]{:S(2)}, u32[]{:S(2)}) collective-permute-start(bf16[352,256]{1,0:T(8,128)(2,1)S(1)} %get-tuple-element.18.a0), channel_id=1, source_target_pairs={{3,0},{0,1},{1,2},{2,3},{7,4},{4,5},{5,6},{6,7},{11,8},{8,9},{9,10... | collective-permute-start | bytes 540680 | tf_op jit(solution)/shard_map/ppermute | solution.py:175
  18.6 12.1 %collective-permute-start.5 = (bf16[352,256]{1,0:T(8,128)(2,1)S(1)}, bf16[352,256]{1,0:T(8,128)(2,1)S(1)}, u32[]{:S(2)}, u32[]{:S(2)}) collective-permute-start(bf16[352,256]{1,0:T(8,128)(2,1)S(1)} %get-tuple-element.19.b0), channel_id=1, source_target_pairs={{1,0},{2,1},{3,2},{0,3},{5,4},{6,5},{7,6},{4,7},{9,8},{10,9},{11,1... | collective-permute-start | bytes 540680 | tf_op jit(solution)/shard_map/ppermute | solution.py:175
  22.9 9.7 %collective-permute-start.1 = (bf16[352,256]{1,0:T(8,128)(2,1)S(1)}, bf16[352,256]{1,0:T(8,128)(2,1)S(1)}, u32[]{:S(2)}, u32[]{:S(2)}) collective-permute-start(bf16[352,256]{1,0:T(8,128)(2,1)S(1)} %collective-permute-done.a1), channel_id=1, source_target_pairs={{1,0},{2,1},{3,2},{0,3},{5,4},{6,5},{7,6},{4,7},{9,8},{10,9},{11,1... | collective-permute-start | bytes 540680 | tf_op jit(solution)/shard_map/ppermute | solution.py:175
  26.7 8.6 %collective-permute-start.3 = (bf16[352,256]{1,0:T(8,128)(2,1)S(1)}, bf16[352,256]{1,0:T(8,128)(2,1)S(1)}, u32[]{:S(2)}, u32[]{:S(2)}) collective-permute-start(bf16[352,256]{1,0:T(8,128)(2,1)S(1)} %collective-permute-done.2.b3), channel_id=1, source_target_pairs={{3,0},{0,1},{1,2},{2,3},{7,4},{4,5},{5,6},{6,7},{11,8},{8,9},{9,10... | collective-permute-start | bytes 540680 | tf_op jit(solution)/shard_map/ppermute | solution.py:175
  27.2 8.1 %copy-start = (bf16[2048,2560]{1,0:T(8,128)(2,1)S(1)}, bf16[2048,2560]{1,0:T(8,128)(2,1)}, u32[]{:S(2)}) copy-start(bf16[2048,2560]{1,0:T(8,128)(2,1)} %adj_ref.1) | copy-start | bytes 31457284
  27.2 8.2 %copy-start.1 = (s32[16,20]{1,0:T(8,128)S(1)}, s32[16,20]{1,0:T(8,128)}, u32[]{:S(2)}) copy-start(s32[16,20]{1,0:T(8,128)} %mask_ref.1) | copy-start | bytes 3844
  27.4 14.4 %collective-permute-start.8 = (bf16[768,128]{1,0:T(8,128)(2,1)S(1)}, bf16[768,128]{1,0:T(8,128)(2,1)S(1)}, u32[]{:S(2)}, u32[]{:S(2)}) collective-permute-start(bf16[768,128]{1,0:T(8,128)(2,1)S(1)} %get-tuple-element.25.b0), channel_id=1, source_target_pairs={{3,0},{0,1},{1,2},{2,3},{7,4},{4,5},{5,6},{6,7},{11,8},{8,9},{9,10... | collective-permute-start | bytes 589832 | tf_op jit(solution)/shard_map/ppermute | solution.py:175
  30.1 11.7 %collective-permute-start.6 = (bf16[768,128]{1,0:T(8,128)(2,1)S(1)}, bf16[768,128]{1,0:T(8,128)(2,1)S(1)}, u32[]{:S(2)}, u32[]{:S(2)}) collective-permute-start(bf16[768,128]{1,0:T(8,128)(2,1)S(1)} %get-tuple-element.25.b0), channel_id=1, source_target_pairs={{1,0},{2,1},{3,2},{0,3},{5,4},{6,5},{7,6},{4,7},{9,8},{10,9},{11,1... | collective-permute-start | bytes 589832 | tf_op jit(solution)/shard_map/ppermute | solution.py:175
  30.7 10.0 %collective-permute-start.7 = (bf16[256,128]{1,0:T(8,128)(2,1)S(1)}, bf16[256,128]{1,0:T(8,128)(2,1)S(1)}, u32[]{:S(2)}, u32[]{:S(2)}) collective-permute-start(bf16[256,128]{1,0:T(8,128)(2,1)S(1)} %get-tuple-element.17._), channel_id=1, source_target_pairs={{2,0},{3,1},{0,2},{1,3},{6,4},{7,5},{4,6},{5,7},{10,8},{11,9},{8,1... | collective-permute-start | bytes 196616 | tf_op jit(solution)/shard_map/ppermute | solution.py:175
  32.7 12.6 %collective-permute-start.9 = (bf16[512,128]{1,0:T(8,128)(2,1)S(1)}, bf16[512,128]{1,0:T(8,128)(2,1)S(1)}, u32[]{:S(2)}, u32[]{:S(2)}) collective-permute-start(bf16[512,128]{1,0:T(8,128)(2,1)S(1)} %get-tuple-element.26), channel_id=1, source_target_pairs={{2,0},{3,1},{0,2},{1,3},{6,4},{7,5},{4,6},{5,7},{10,8},{11,9},{8,1... | collective-permute-start | bytes 393224 | tf_op jit(solution)/shard_map/ppermute | solution.py:175

commit v4 on v3

--- a/solution.py
+++ b/solution.py
@@ -76,18 +76,23 @@
     whole_ref[half:, :] = far
 
 
-def prep_kernel(mask_ref, adj_ref, _, __, ___, _a, _b, masked_ref, scale_ref):
+def prep_kernel(mask_ref, adj_ref, far_ref, _, __, ___, masked_ref, scale_ref, later_ref):
+    later_ref[...] = far_ref[...]
     rows, cols = masked_ref.shape
+    step = 16
     for i in range(rows // TILE):
-        part = pl.ds(i * TILE, TILE)
-        total = jnp.zeros((TILE, TILE), F32)
-        for t in range(cols // TILE):
-            keep = mask_ref[i, t].astype(F32).astype(BF)
-            tile = adj_ref[part, t * TILE : (t + 1) * TILE] * keep
-            masked_ref[part, t * TILE : (t + 1) * TILE] = tile
-            total += tile.astype(F32)
-        scale = 0.9 / (1.0 + jnp.sum(total, axis=1, keepdims=True))
-        scale_ref[part, :] = jnp.broadcast_to(scale, (TILE, scale_ref.shape[1]))
+        keep = [jnp.full((1, TILE), mask_ref[i, t].astype(F32), F32) for t in range(cols // TILE)]
+        keep = jnp.concatenate(keep, axis=1).astype(BF)
+        for begin in range(i * TILE, (i + 1) * TILE, step):
+            part = pl.ds(begin, step)
+            held = adj_ref[part, :] * keep
+            masked_ref[part, :] = held
+            wide = held.astype(F32)
+            total = wide[:, :TILE]
+            for t in range(1, cols // TILE):
+                total = total + wide[:, t * TILE : (t + 1) * TILE]
+            scale = 0.9 / (1.0 + jnp.sum(total, axis=1, keepdims=True))
+            scale_ref[part, :] = jnp.broadcast_to(scale, (step, scale_ref.shape[1]))
 
 
 def own_kernel(place_ref, masked_ref, a0, a1, a2, a3, b0, b1, b2, b3, sums_ref, rest_ref, weight_ref, init_ref):
@@ -222,18 +227,18 @@
     )(in_vmem(arrived.reshape(halo, full)))
     after_all, before_all = ring(whole, 1), ring(whole, 3)
     nears = [whole, after_all, ring(near, 2), before_all]
-    fars = [whole, after_all, ring(far, 2), before_all]
-
-    masked, scale = pl.pallas_call(
+
+    masked, scale, later = pl.pallas_call(
         prep_kernel,
-        out_shape=[pltpu.VMEM((rows, cols), BF), pltpu.VMEM((rows, 128), F32)],
-        in_specs=[smem] + [vmem] * 6,
-        out_specs=[vmem] * 2,
+        out_shape=[pltpu.VMEM((rows, cols), BF), pltpu.VMEM((rows, 128), F32), pltpu.VMEM((halo, 128), BF)],
+        in_specs=[smem] + [vmem] * 5,
+        out_specs=[vmem] * 3,
         compiler_params=params(vmem_limit_bytes=14 * MIB),
         cost_estimate=pl.CostEstimate(flops=4300001000, bytes_accessed=1000, transcendentals=0),
         name="prep",
-    )(tile_mask, adjacency, in_vmem(near), *[in_vmem(packs[k]) for k in (2, 6, 3, 5)])
-
+    )(tile_mask, adjacency, in_vmem(far), *[in_vmem(packs[k]) for k in (2, 3, 5)])
+
+    fars = [whole, after_all, ring(later, 2), before_all]
     sums, rest, turned = pl.pallas_call(
         own_kernel,
         out_shape=[

time: 50.6 us -> 50.2 us (level)
  the two profiles are of different devices: /device:TPU:2 before, /device:TPU:1 now
where the time goes in v4:
time: 50.2 us; the launch traced here: 50 us
  starting transfers between devices  28.9 us (58%)
  Pallas kernels  16.8 us (33%)
  waiting for transfers between devices  4.24 us (8%)
    ppermute x10, starting transfers between devices, ring(): return lax.ppermute(x, 'feat', [((i + shift) % 4, i) for i in range(4)])  15.9 us
    all_to_all x1, starting transfers between devices, local(): lax.all_to_all(outgoing.reshape(peers, slots, full), 'dom', split_axis=0,...  13 us
    pallas_call x1, Pallas kernels, local(): pl.pallas_call(late_kernel, out_shape=jax.ShapeDtypeStruct((width, rows),...  5.15 us
    all_to_all x1, waiting for transfers between devices, local(): lax.all_to_all(outgoing.reshape(peers, slots, full), 'dom', split_axis=0,...  3.46 us
    pallas_call x1, Pallas kernels, local(): pl.pallas_call(early_kernel, out_shape=pltpu.VMEM((rows, full), F32), in_...  3.46 us
    pallas_call x1, Pallas kernels, local(): pl.pallas_call(pick_kernel, out_shape=[pltpu.VMEM((halo, full), BF)] + [p...  2.89 us
    pallas_call x1, Pallas kernels, local(): pl.pallas_call(prep_kernel, out_shape=[pltpu.VMEM((rows, cols), BF), pltp...  2.72 us
    pallas_call x1, Pallas kernels, local(): pl.pallas_call(own_kernel, out_shape=[pltpu.VMEM((rows, full), F32), pltp...  2.44 us
  transfers between devices with their start and end apart: 11, of which 2 were waited for; matrix products, arithmetic and copies ran while one was open for 0% of the time, Pallas kernels for 18%

profile of v4, /device:TPU:1, one launch (start us, length us, event | category | flops | bytes accessed | tf_op | source)
XLA Modules:
  0.0 50.0 jit_solution(10583401991278819612)
XLA Ops:
  0.0 2.9 %pick.1 = (bf16[512,256]{1,0:T(8,128)(2,1)}, bf16[352,256]{1,0:T(8,128)(2,1)S(1)}, bf16[352,256]{1,0:T(8,128)(2,1)S(1)}) custom-call(s32[8,64]{1,0:T(8,128)} %bitcast.12, bf16[64,2048]{1,0:T(8,128)(2,1)} %bitcast.11, bf16[2,64,2048]{2,1,0:T(8,128)(2,1)} %bitcast.10, bf16[3,64,256]{2,1,0:T(8,128)(2,1)} %weight_hbm.1), custom_call_target="tpu_custom_call" | custom-call | tf_op jit(solution)/shard_map/pick/pallas_call | solution.py:199
  2.9 13.0 %all-to-all-start = ((bf16[64,8,256]{2,1,0:T(8,128)(2,1)}), bf16[64,8,256]{2,1,0:T(8,128)(2,1)S(1)}, u32[]{:S(2)}, u32[]{:S(2)}) async-start(bf16[64,8,256]{2,1,0:T(8,128)(2,1)} %bitcast.4), calls=%async_computation | async-start | bytes 524288 | tf_op jit(solution)/shard_map/all_to_all | solution.py:218
  15.9 2.8 %collective-permute-start = (bf16[352,256]{1,0:T(8,128)(2,1)S(1)}, bf16[352,256]{1,0:T(8,128)(2,1)S(1)}, u32[]{:S(2)}, u32[]{:S(2)}) collective-permute-start(bf16[352,256]{1,0:T(8,128)(2,1)S(1)} %get-tuple-element.19.a0), channel_id=1, source_target_pairs={{1,0},{2,1},{3,2},{0,3},{5,4},{6,5},{7,6},{4,7},{9,8},{10,9},{11,1... | collective-permute-start | bytes 540680 | tf_op jit(solution)/shard_map/ppermute | solution.py:180
  18.7 0.0 collective-permute-start.4
  18.7 0.0 collective-permute-start.2
  18.7 2.7 %collective-permute-start.3 = (bf16[352,256]{1,0:T(8,128)(2,1)S(1)}, bf16[352,256]{1,0:T(8,128)(2,1)S(1)}, u32[]{:S(2)}, u32[]{:S(2)}) collective-permute-start(bf16[352,256]{1,0:T(8,128)(2,1)S(1)} %get-tuple-element.20.b0), channel_id=1, source_target_pairs={{1,0},{2,1},{3,2},{0,3},{5,4},{6,5},{7,6},{4,7},{9,8},{10,9},{11,1... | collective-permute-start | bytes 540680 | tf_op jit(solution)/shard_map/ppermute | solution.py:180
  21.4 0.8 %collective-permute-done.a1 = bf16[352,256]{1,0:T(8,128)(2,1)S(1)} collective-permute-done((bf16[352,256]{1,0:T(8,128)(2,1)S(1)}, bf16[352,256]{1,0:T(8,128)(2,1)S(1)}, u32[]{:S(2)}, u32[]{:S(2)}) %collective-permute-start) | collective-permute-done | bytes 180256 | tf_op jit(solution)/shard_map/ppermute | solution.py:180
  22.2 3.4 %collective-permute-start.1 = (bf16[352,256]{1,0:T(8,128)(2,1)S(1)}, bf16[352,256]{1,0:T(8,128)(2,1)S(1)}, u32[]{:S(2)}, u32[]{:S(2)}) collective-permute-start(bf16[352,256]{1,0:T(8,128)(2,1)S(1)} %collective-permute-done.a1), channel_id=1, source_target_pairs={{1,0},{2,1},{3,2},{0,3},{5,4},{6,5},{7,6},{4,7},{9,8},{10,9},{11,1... | collective-permute-start | bytes 540680 | tf_op jit(solution)/shard_map/ppermute | solution.py:180
  25.6 0.0 collective-permute-done.4.b3
  25.6 0.0 collective-permute-start.5
  25.6 3.5 %all-to-all-done = bf16[64,8,256]{2,1,0:T(8,128)(2,1)S(1)} async-done(((bf16[64,8,256]{2,1,0:T(8,128)(2,1)}), bf16[64,8,256]{2,1,0:T(8,128)(2,1)S(1)}, u32[]{:S(2)}, u32[]{:S(2)}) %all-to-all-start) | async-done | bytes 262176 | tf_op jit(solution)/shard_map/all_to_all | solution.py:218
  29.1 0.0 copy-start
  29.1 0.0 copy-start.1
  29.1 0.2 compact.1
  29.3 1.4 %collective-permute-start.8 = (bf16[768,128]{1,0:T(8,128)(2,1)S(1)}, bf16[768,128]{1,0:T(8,128)(2,1)S(1)}, u32[]{:S(2)}, u32[]{:S(2)}) collective-permute-start(bf16[768,128]{1,0:T(8,128)(2,1)S(1)} %get-tuple-element.26.b0), channel_id=1, source_target_pairs={{3,0},{0,1},{1,2},{2,3},{7,4},{4,5},{5,6},{6,7},{11,8},{8,9},{9,10... | collective-permute-start | bytes 589832 | tf_op jit(solution)/shard_map/ppermute | solution.py:180
  30.6 0.0 collective-permute-done.2.__.a3
  30.6 1.5 %collective-permute-start.6 = (bf16[768,128]{1,0:T(8,128)(2,1)S(1)}, bf16[768,128]{1,0:T(8,128)(2,1)S(1)}, u32[]{:S(2)}, u32[]{:S(2)}) collective-permute-start(bf16[768,128]{1,0:T(8,128)(2,1)S(1)} %get-tuple-element.26.b0), channel_id=1, source_target_pairs={{1,0},{2,1},{3,2},{0,3},{5,4},{6,5},{7,6},{4,7},{9,8},{10,9},{11,1... | collective-permute-start | bytes 589832 | tf_op jit(solution)/shard_map/ppermute | solution.py:180
  32.2 0.0 collective-permute-done.3.___.b1
  32.2 1.5 %collective-permute-start.7 = (bf16[256,128]{1,0:T(8,128)(2,1)S(1)}, bf16[256,128]{1,0:T(8,128)(2,1)S(1)}, u32[]{:S(2)}, u32[]{:S(2)}) collective-permute-start(bf16[256,128]{1,0:T(8,128)(2,1)S(1)} %get-tuple-element.27), channel_id=1, source_target_pairs={{2,0},{3,1},{0,2},{1,3},{6,4},{7,5},{4,6},{5,7},{10,8},{11,9},{8,1... | collective-permute-start | bytes 196616 | tf_op jit(solution)/shard_map/ppermute | solution.py:180
  33.7 0.0 collective-permute-done.1._.a2
  33.7 0.0 copy-done
  33.7 0.0 copy-done.1
  33.7 2.7 %prep.1 = (bf16[2048,2560]{1,0:T(8,128)(2,1)S(1)}, f32[2048,128]{1,0:T(8,128)S(1)}, bf16[512,128]{1,0:T(8,128)(2,1)S(1)}) custom-call(s32[16,20]{1,0:T(8,128)S(1)} %copy-done.1, bf16[2048,2560]{1,0:T(8,128)(2,1)S(1)} %copy-done, bf16[512,128]{1,0:T(8,128)(2,1)S(1)} %get-tuple-element.18.far_ref, bf16[352,256]{1,0:T(8,128)(2,1)S(1)} %collective-permute-done.1._.a2, ...), custom_call_target="tpu_custom_call" | custom-call | flops 4300000768 | bytes 1000 | tf_op jit(solution)/shard_map/prep/pallas_call | solution.py:231
  36.5 2.5 %collective-permute-start.9 = (bf16[512,128]{1,0:T(8,128)(2,1)S(1)}, bf16[512,128]{1,0:T(8,128)(2,1)S(1)}, u32[]{:S(2)}, u32[]{:S(2)}) collective-permute-start(bf16[512,128]{1,0:T(8,128)(2,1)S(1)} %get-tuple-element.28), channel_id=1, source_target_pairs={{2,0},{3,1},{0,2},{1,3},{6,4},{7,5},{4,6},{5,7},{10,8},{11,9},{8,1... | collective-permute-start | bytes 393224 | tf_op jit(solution)/shard_map/ppermute | solution.py:180
  38.9 0.0 collective-permute-done.5.b2
  38.9 2.4 %own.1 = (f32[2048,256]{1,0:T(8,128)S(1)}, f32[2048,256]{1,0:T(8,128)S(1)}, bf16[3,256,256]{2,1,0:T(8,128)(2,1)S(1)}) custom-call(s32[1]{0:T(128)} %bitcast.6.place_ref, bf16[2048,2560]{1,0:T(8,128)(2,1)S(1)} %get-tuple-element.21.masked_ref, bf16[352,256]{1,0:T(8,128)(2,1)S(1)} %get-tuple-element.19.a0, bf16[352,256]{1,0:T(8,128)(2,1)S(1)} %collective-permute-done.a1, ...), custom_call_target="tpu_custom_call" | custom-call | flops 2100001024 | bytes 1000 | tf_op jit(solution)/shard_map/own/pallas_call | solution.py:242
  41.4 0.0 collective-permute-done.7.b2
  41.4 0.0 collective-permute-done.8.b3
  41.4 0.0 collective-permute-done.6.b1
  41.4 3.5 %early.1.sums_ref = f32[2048,256]{1,0:T(8,128)S(1)} custom-call(bf16[2048,2560]{1,0:T(8,128)(2,1)S(1)} %get-tuple-element.21.masked_ref, f32[2048,128]{1,0:T(8,128)S(1)} %get-tuple-element.22.scale_ref, f32[2048,256]{1,0:T(8,128)S(1)} %get-tuple-element.23.sums_ref, f32[2048,256]{1,0:T(8,128)S(1)} %get-tuple-element.24.rest_ref, ...), custom_call_target="tpu_custom_call" | custom-call | flops 1000 | bytes 1000 | tf_op jit(solution)/shard_map/early/pallas_call | solution.py:257
  44.9 0.0 collective-permute-done.9.b2
  44.9 5.1 %late.1 = bf16[64,2048]{1,0:T(8,128)(2,1)} custom-call(bf16[2048,2560]{1,0:T(8,128)(2,1)S(1)} %get-tuple-element.21.masked_ref, f32[2048,128]{1,0:T(8,128)S(1)} %get-tuple-element.22.scale_ref, f32[2048,256]{1,0:T(8,128)S(1)} %early.1.sums_ref, f32[2048,256]{1,0:T(8,128)S(1)} %get-tuple-element.24.rest_ref, ...), custom_call_target="tpu_custom_call" | custom-call | tf_op jit(solution)/shard_map/late/pallas_call | solution.py:268
Async XLA Ops:
  2.9 26.2 %all-to-all-start = ((bf16[64,8,256]{2,1,0:T(8,128)(2,1)}), bf16[64,8,256]{2,1,0:T(8,128)(2,1)S(1)}, u32[]{:S(2)}, u32[]{:S(2)}) async-start(bf16[64,8,256]{2,1,0:T(8,128)(2,1)} %bitcast.4), calls=%async_computation | async-start | bytes 524288 | tf_op jit(solution)/shard_map/all_to_all | solution.py:218
  15.9 6.3 %collective-permute-start = (bf16[352,256]{1,0:T(8,128)(2,1)S(1)}, bf16[352,256]{1,0:T(8,128)(2,1)S(1)}, u32[]{:S(2)}, u32[]{:S(2)}) collective-permute-start(bf16[352,256]{1,0:T(8,128)(2,1)S(1)} %get-tuple-element.19.a0), channel_id=1, source_target_pairs={{1,0},{2,1},{3,2},{0,3},{5,4},{6,5},{7,6},{4,7},{9,8},{10,9},{11,1... | collective-permute-start | bytes 540680 | tf_op jit(solution)/shard_map/ppermute | solution.py:180
  18.7 6.9 %collective-permute-start.4 = (bf16[352,256]{1,0:T(8,128)(2,1)S(1)}, bf16[352,256]{1,0:T(8,128)(2,1)S(1)}, u32[]{:S(2)}, u32[]{:S(2)}) collective-permute-start(bf16[352,256]{1,0:T(8,128)(2,1)S(1)} %get-tuple-element.20.b0), channel_id=1, source_target_pairs={{3,0},{0,1},{1,2},{2,3},{7,4},{4,5},{5,6},{6,7},{11,8},{8,9},{9,10... | collective-permute-start | bytes 540680 | tf_op jit(solution)/shard_map/ppermute | solution.py:180
  18.7 11.9 %collective-permute-start.2 = (bf16[352,256]{1,0:T(8,128)(2,1)S(1)}, bf16[352,256]{1,0:T(8,128)(2,1)S(1)}, u32[]{:S(2)}, u32[]{:S(2)}) collective-permute-start(bf16[352,256]{1,0:T(8,128)(2,1)S(1)} %get-tuple-element.19.a0), channel_id=1, source_target_pairs={{3,0},{0,1},{1,2},{2,3},{7,4},{4,5},{5,6},{6,7},{11,8},{8,9},{9,10... | collective-permute-start | bytes 540680 | tf_op jit(solution)/shard_map/ppermute | solution.py:180
  18.7 13.4 %collective-permute-start.3 = (bf16[352,256]{1,0:T(8,128)(2,1)S(1)}, bf16[352,256]{1,0:T(8,128)(2,1)S(1)}, u32[]{:S(2)}, u32[]{:S(2)}) collective-permute-start(bf16[352,256]{1,0:T(8,128)(2,1)S(1)} %get-tuple-element.20.b0), channel_id=1, source_target_pairs={{1,0},{2,1},{3,2},{0,3},{5,4},{6,5},{7,6},{4,7},{9,8},{10,9},{11,1... | collective-permute-start | bytes 540680 | tf_op jit(solution)/shard_map/ppermute | solution.py:180
  22.2 11.5 %collective-permute-start.1 = (bf16[352,256]{1,0:T(8,128)(2,1)S(1)}, bf16[352,256]{1,0:T(8,128)(2,1)S(1)}, u32[]{:S(2)}, u32[]{:S(2)}) collective-permute-start(bf16[352,256]{1,0:T(8,128)(2,1)S(1)} %collective-permute-done.a1), channel_id=1, source_target_pairs={{1,0},{2,1},{3,2},{0,3},{5,4},{6,5},{7,6},{4,7},{9,8},{10,9},{11,1... | collective-permute-start | bytes 540680 | tf_op jit(solution)/shard_map/ppermute | solution.py:180
  25.6 13.4 %collective-permute-start.5 = (bf16[352,256]{1,0:T(8,128)(2,1)S(1)}, bf16[352,256]{1,0:T(8,128)(2,1)S(1)}, u32[]{:S(2)}, u32[]{:S(2)}) collective-permute-start(bf16[352,256]{1,0:T(8,128)(2,1)S(1)} %collective-permute-done.4.b3), channel_id=1, source_target_pairs={{3,0},{0,1},{1,2},{2,3},{7,4},{4,5},{5,6},{6,7},{11,8},{8,9},{9,10... | collective-permute-start | bytes 540680 | tf_op jit(solution)/shard_map/ppermute | solution.py:180
  29.1 4.7 %copy-start = (bf16[2048,2560]{1,0:T(8,128)(2,1)S(1)}, bf16[2048,2560]{1,0:T(8,128)(2,1)}, u32[]{:S(2)}) copy-start(bf16[2048,2560]{1,0:T(8,128)(2,1)} %adj_ref.1) | copy-start | bytes 31457284
  29.1 4.7 %copy-start.1 = (s32[16,20]{1,0:T(8,128)S(1)}, s32[16,20]{1,0:T(8,128)}, u32[]{:S(2)}) copy-start(s32[16,20]{1,0:T(8,128)} %mask_ref.1) | copy-start | bytes 3844
  29.3 12.1 %collective-permute-start.8 = (bf16[768,128]{1,0:T(8,128)(2,1)S(1)}, bf16[768,128]{1,0:T(8,128)(2,1)S(1)}, u32[]{:S(2)}, u32[]{:S(2)}) collective-permute-start(bf16[768,128]{1,0:T(8,128)(2,1)S(1)} %get-tuple-element.26.b0), channel_id=1, source_target_pairs={{3,0},{0,1},{1,2},{2,3},{7,4},{4,5},{5,6},{6,7},{11,8},{8,9},{9,10... | collective-permute-start | bytes 589832 | tf_op jit(solution)/shard_map/ppermute | solution.py:180
  30.6 10.8 %collective-permute-start.6 = (bf16[768,128]{1,0:T(8,128)(2,1)S(1)}, bf16[768,128]{1,0:T(8,128)(2,1)S(1)}, u32[]{:S(2)}, u32[]{:S(2)}) collective-permute-start(bf16[768,128]{1,0:T(8,128)(2,1)S(1)} %get-tuple-element.26.b0), channel_id=1, source_target_pairs={{1,0},{2,1},{3,2},{0,3},{5,4},{6,5},{7,6},{4,7},{9,8},{10,9},{11,1... | collective-permute-start | bytes 589832 | tf_op jit(solution)/shard_map/ppermute | solution.py:180
  32.2 9.2 %collective-permute-start.7 = (bf16[256,128]{1,0:T(8,128)(2,1)S(1)}, bf16[256,128]{1,0:T(8,128)(2,1)S(1)}, u32[]{:S(2)}, u32[]{:S(2)}) collective-permute-start(bf16[256,128]{1,0:T(8,128)(2,1)S(1)} %get-tuple-element.27), channel_id=1, source_target_pairs={{2,0},{3,1},{0,2},{1,3},{6,4},{7,5},{4,6},{5,7},{10,8},{11,9},{8,1... | collective-permute-start | bytes 196616 | tf_op jit(solution)/shard_map/ppermute | solution.py:180
  36.5 8.4 %collective-permute-start.9 = (bf16[512,128]{1,0:T(8,128)(2,1)S(1)}, bf16[512,128]{1,0:T(8,128)(2,1)S(1)}, u32[]{:S(2)}, u32[]{:S(2)}) collective-permute-start(bf16[512,128]{1,0:T(8,128)(2,1)S(1)} %get-tuple-element.28), channel_id=1, source_target_pairs={{2,0},{3,1},{0,2},{1,3},{6,4},{7,5},{4,6},{5,7},{10,8},{11,9},{8,1... | collective-permute-start | bytes 393224 | tf_op jit(solution)/shard_map/ppermute | solution.py:180

commit v5 on v4

--- a/solution.py
+++ b/solution.py
@@ -123,7 +123,7 @@
     rest_ref[...] = 0.1 * init_ref[...].astype(F32)
 
 
-def finish(depth, acc_ref, scale_ref, rest_ref, weight_ref, made_ref):
+def finish(depth, acc_ref, scale_ref, rest_ref, weight_ref, made_ref, send=None):
     step = 256
     beta = math.log(0.5 / (depth + 1) + 1.0)
     for begin in range(0, acc_ref.shape[0], step):
@@ -135,6 +135,7 @@
             product = jnp.dot(low, weight_ref[depth, :, :128], preferred_element_type=F32)
             made = jnp.maximum((1.0 - beta) * support[:, :128] + beta * product, 0.0)
             made_ref[:, part] = made.T[:64].astype(BF)
+            send(begin // step).start()
         else:
             product = jnp.dot(low, weight_ref[depth], preferred_element_type=F32)
             made = jnp.maximum((1.0 - beta) * support + beta * product, 0.0).astype(BF)
@@ -158,7 +159,7 @@
         next_ref[whole, :] = jnp.dot(masked_ref[whole, :rows], made[...], preferred_element_type=F32)
 
 
-def late_kernel(masked_ref, scale_ref, sums_ref, rest_ref, weight_ref, b0, b1, b2, b3, out_ref, joined, acc_ref):
+def late_kernel(masked_ref, scale_ref, sums_ref, rest_ref, weight_ref, b0, b1, b2, b3, out_hbm, joined, acc_ref, out_ref, sems):
     rows, cols = masked_ref.shape
     half = (cols - rows) // 2
     packs = (b0[half:, :], b1[half:, :], b2[...], b3[half:, :])
@@ -173,7 +174,16 @@
     for begin in range(0, rows, block):
         whole = pl.ds(begin, block)
         acc_ref[whole, :] = jnp.dot(masked_ref[whole, :], joined[...], preferred_element_type=F32)
-    finish(2, acc_ref, scale_ref, rest_ref, weight_ref, out_ref)
+    count = sems.shape[0]
+    size = rows // count
+
+    def send(i):
+        part = pl.ds(i * size, size)
+        return pltpu.make_async_copy(out_ref.at[:, part], out_hbm.at[:, part], sems.at[i])
+
+    finish(2, acc_ref, scale_ref, rest_ref, weight_ref, out_ref, send)
+    for i in range(count):
+        send(i).wait()
 
 
 def ring(x, shift):
@@ -269,8 +279,13 @@
         late_kernel,
         out_shape=jax.ShapeDtypeStruct((width, rows), BF),
         in_specs=[vmem] * 9,
-        out_specs=vmem,
-        scratch_shapes=[pltpu.VMEM((cols, full), BF), pltpu.VMEM((rows, full), F32)],
+        out_specs=hbm,
+        scratch_shapes=[
+            pltpu.VMEM((cols, full), BF),
+            pltpu.VMEM((rows, full), F32),
+            pltpu.VMEM((width, rows), BF),
+            pltpu.SemaphoreType.DMA((rows // 256,)),
+        ],
         compiler_params=params(vmem_limit_bytes=10 * MIB),
         name="late",
     )(*[in_vmem(x) for x in (masked, scale, sums, rest, turned, *fars)])

time: 50.2 us -> 50.4 us (level)
  no operation moved by 1% of the time
where the time goes in v5:
time: 50.4 us; the launch traced here: 50.2 us
  starting transfers between devices  28.9 us (57%)
  Pallas kernels  16.8 us (33%)
  waiting for transfers between devices  4.24 us (8%)
    ppermute x10, starting transfers between devices, ring(): return lax.ppermute(x, 'feat', [((i + shift) % 4, i) for i in range(4)])  15.9 us
    all_to_all x1, starting transfers between devices, local(): lax.all_to_all(outgoing.reshape(peers, slots, full), 'dom', split_axis=0,...  13 us
    pallas_call x1, Pallas kernels, local(): pl.pallas_call(late_kernel, out_shape=jax.ShapeDtypeStruct((width, rows),...  5.14 us
    all_to_all x1, waiting for transfers between devices, local(): lax.all_to_all(outgoing.reshape(peers, slots, full), 'dom', split_axis=0,...  3.46 us
    pallas_call x1, Pallas kernels, local(): pl.pallas_call(early_kernel, out_shape=pltpu.VMEM((rows, full), F32), in_...  3.46 us
    pallas_call x1, Pallas kernels, local(): pl.pallas_call(pick_kernel, out_shape=[pltpu.VMEM((halo, full), BF)] + [p...  2.89 us
    pallas_call x1, Pallas kernels, local(): pl.pallas_call(prep_kernel, out_shape=[pltpu.VMEM((rows, cols), BF), pltp...  2.72 us
    pallas_call x1, Pallas kernels, local(): pl.pallas_call(own_kernel, out_shape=[pltpu.VMEM((rows, full), F32), pltp...  2.44 us
  transfers between devices with their start and end apart: 11, of which 2 were waited for; matrix products, arithmetic and copies ran while one was open for 0% of the time, Pallas kernels for 18%

profile of v5, /device:TPU:1, one launch (start us, length us, event | category | flops | bytes accessed | tf_op | source)
XLA Modules:
  0.0 50.2 jit_solution(16376474078481620640)
XLA Ops:
  0.0 2.9 %pick.1 = (bf16[512,256]{1,0:T(8,128)(2,1)}, bf16[352,256]{1,0:T(8,128)(2,1)S(1)}, bf16[352,256]{1,0:T(8,128)(2,1)S(1)}) custom-call(s32[8,64]{1,0:T(8,128)} %bitcast.12, bf16[64,2048]{1,0:T(8,128)(2,1)} %bitcast.11, bf16[2,64,2048]{2,1,0:T(8,128)(2,1)} %bitcast.10, bf16[3,64,256]{2,1,0:T(8,128)(2,1)} %weight_hbm.1), custom_call_target="tpu_custom_call" | custom-call | tf_op jit(solution)/shard_map/pick/pallas_call | solution.py:209
  2.9 13.0 %all-to-all-start = ((bf16[64,8,256]{2,1,0:T(8,128)(2,1)}), bf16[64,8,256]{2,1,0:T(8,128)(2,1)S(1)}, u32[]{:S(2)}, u32[]{:S(2)}) async-start(bf16[64,8,256]{2,1,0:T(8,128)(2,1)} %bitcast.4), calls=%async_computation | async-start | bytes 524288 | tf_op jit(solution)/shard_map/all_to_all | solution.py:228
  15.9 2.8 %collective-permute-start = (bf16[352,256]{1,0:T(8,128)(2,1)S(1)}, bf16[352,256]{1,0:T(8,128)(2,1)S(1)}, u32[]{:S(2)}, u32[]{:S(2)}) collective-permute-start(bf16[352,256]{1,0:T(8,128)(2,1)S(1)} %get-tuple-element.19.a0), channel_id=1, source_target_pairs={{1,0},{2,1},{3,2},{0,3},{5,4},{6,5},{7,6},{4,7},{9,8},{10,9},{11,1... | collective-permute-start | bytes 540680 | tf_op jit(solution)/shard_map/ppermute | solution.py:190
  18.7 0.0 collective-permute-start.4
  18.7 0.0 collective-permute-start.2
  18.7 2.7 %collective-permute-start.3 = (bf16[352,256]{1,0:T(8,128)(2,1)S(1)}, bf16[352,256]{1,0:T(8,128)(2,1)S(1)}, u32[]{:S(2)}, u32[]{:S(2)}) collective-permute-start(bf16[352,256]{1,0:T(8,128)(2,1)S(1)} %get-tuple-element.20.b0), channel_id=1, source_target_pairs={{1,0},{2,1},{3,2},{0,3},{5,4},{6,5},{7,6},{4,7},{9,8},{10,9},{11,1... | collective-permute-start | bytes 540680 | tf_op jit(solution)/shard_map/ppermute | solution.py:190
  21.4 0.8 %collective-permute-done.a1 = bf16[352,256]{1,0:T(8,128)(2,1)S(1)} collective-permute-done((bf16[352,256]{1,0:T(8,128)(2,1)S(1)}, bf16[352,256]{1,0:T(8,128)(2,1)S(1)}, u32[]{:S(2)}, u32[]{:S(2)}) %collective-permute-start) | collective-permute-done | bytes 180256 | tf_op jit(solution)/shard_map/ppermute | solution.py:190
  22.2 3.4 %collective-permute-start.1 = (bf16[352,256]{1,0:T(8,128)(2,1)S(1)}, bf16[352,256]{1,0:T(8,128)(2,1)S(1)}, u32[]{:S(2)}, u32[]{:S(2)}) collective-permute-start(bf16[352,256]{1,0:T(8,128)(2,1)S(1)} %collective-permute-done.a1), channel_id=1, source_target_pairs={{1,0},{2,1},{3,2},{0,3},{5,4},{6,5},{7,6},{4,7},{9,8},{10,9},{11,1... | collective-permute-start | bytes 540680 | tf_op jit(solution)/shard_map/ppermute | solution.py:190
  25.6 0.0 collective-permute-done.4.b3
  25.6 0.0 collective-permute-start.5
  25.6 3.5 %all-to-all-done = bf16[64,8,256]{2,1,0:T(8,128)(2,1)S(1)} async-done(((bf16[64,8,256]{2,1,0:T(8,128)(2,1)}), bf16[64,8,256]{2,1,0:T(8,128)(2,1)S(1)}, u32[]{:S(2)}, u32[]{:S(2)}) %all-to-all-start) | async-done | bytes 262176 | tf_op jit(solution)/shard_map/all_to_all | solution.py:228
  29.1 0.0 copy-start
  29.1 0.0 copy-start.1
  29.1 0.2 compact.1
  29.3 1.4 %collective-permute-start.8 = (bf16[768,128]{1,0:T(8,128)(2,1)S(1)}, bf16[768,128]{1,0:T(8,128)(2,1)S(1)}, u32[]{:S(2)}, u32[]{:S(2)}) collective-permute-start(bf16[768,128]{1,0:T(8,128)(2,1)S(1)} %get-tuple-element.26.b0), channel_id=1, source_target_pairs={{3,0},{0,1},{1,2},{2,3},{7,4},{4,5},{5,6},{6,7},{11,8},{8,9},{9,10... | collective-permute-start | bytes 589832 | tf_op jit(solution)/shard_map/ppermute | solution.py:190
  30.6 0.0 collective-permute-done.2.__.a3
  30.6 1.5 %collective-permute-start.6 = (bf16[768,128]{1,0:T(8,128)(2,1)S(1)}, bf16[768,128]{1,0:T(8,128)(2,1)S(1)}, u32[]{:S(2)}, u32[]{:S(2)}) collective-permute-start(bf16[768,128]{1,0:T(8,128)(2,1)S(1)} %get-tuple-element.26.b0), channel_id=1, source_target_pairs={{1,0},{2,1},{3,2},{0,3},{5,4},{6,5},{7,6},{4,7},{9,8},{10,9},{11,1... | collective-permute-start | bytes 589832 | tf_op jit(solution)/shard_map/ppermute | solution.py:190
  32.2 0.0 collective-permute-done.3.___.b1
  32.2 1.5 %collective-permute-start.7 = (bf16[256,128]{1,0:T(8,128)(2,1)S(1)}, bf16[256,128]{1,0:T(8,128)(2,1)S(1)}, u32[]{:S(2)}, u32[]{:S(2)}) collective-permute-start(bf16[256,128]{1,0:T(8,128)(2,1)S(1)} %get-tuple-element.27), channel_id=1, source_target_pairs={{2,0},{3,1},{0,2},{1,3},{6,4},{7,5},{4,6},{5,7},{10,8},{11,9},{8,1... | collective-permute-start | bytes 196616 | tf_op jit(solution)/shard_map/ppermute | solution.py:190
  33.7 0.0 collective-permute-done.1._.a2
  33.7 0.0 copy-done
  33.7 0.0 copy-done.1
  33.7 2.7 %prep.1 = (bf16[2048,2560]{1,0:T(8,128)(2,1)S(1)}, f32[2048,128]{1,0:T(8,128)S(1)}, bf16[512,128]{1,0:T(8,128)(2,1)S(1)}) custom-call(s32[16,20]{1,0:T(8,128)S(1)} %copy-done.1, bf16[2048,2560]{1,0:T(8,128)(2,1)S(1)} %copy-done, bf16[512,128]{1,0:T(8,128)(2,1)S(1)} %get-tuple-element.18.far_ref, bf16[352,256]{1,0:T(8,128)(2,1)S(1)} %collective-permute-done.1._.a2, ...), custom_call_target="tpu_custom_call" | custom-call | flops 4300000768 | bytes 1000 | tf_op jit(solution)/shard_map/prep/pallas_call | solution.py:241
  36.5 2.5 %collective-permute-start.9 = (bf16[512,128]{1,0:T(8,128)(2,1)S(1)}, bf16[512,128]{1,0:T(8,128)(2,1)S(1)}, u32[]{:S(2)}, u32[]{:S(2)}) collective-permute-start(bf16[512,128]{1,0:T(8,128)(2,1)S(1)} %get-tuple-element.28), channel_id=1, source_target_pairs={{2,0},{3,1},{0,2},{1,3},{6,4},{7,5},{4,6},{5,7},{10,8},{11,9},{8,1... | collective-permute-start | bytes 393224 | tf_op jit(solution)/shard_map/ppermute | solution.py:190
  38.9 0.0 collective-permute-done.5.b2
  38.9 2.4 %own.1 = (f32[2048,256]{1,0:T(8,128)S(1)}, f32[2048,256]{1,0:T(8,128)S(1)}, bf16[3,256,256]{2,1,0:T(8,128)(2,1)S(1)}) custom-call(s32[1]{0:T(128)} %bitcast.6.place_ref, bf16[2048,2560]{1,0:T(8,128)(2,1)S(1)} %get-tuple-element.21.masked_ref, bf16[352,256]{1,0:T(8,128)(2,1)S(1)} %get-tuple-element.19.a0, bf16[352,256]{1,0:T(8,128)(2,1)S(1)} %collective-permute-done.a1, ...), custom_call_target="tpu_custom_call" | custom-call | flops 2100001024 | bytes 1000 | tf_op jit(solution)/shard_map/own/pallas_call | solution.py:252
  41.4 0.0 collective-permute-done.7.b2
  41.4 0.0 collective-permute-done.8.b3
  41.4 0.0 collective-permute-done.6.b1
  41.4 3.5 %early.1.sums_ref = f32[2048,256]{1,0:T(8,128)S(1)} custom-call(bf16[2048,2560]{1,0:T(8,128)(2,1)S(1)} %get-tuple-element.21.masked_ref, f32[2048,128]{1,0:T(8,128)S(1)} %get-tuple-element.22.scale_ref, f32[2048,256]{1,0:T(8,128)S(1)} %get-tuple-element.23.sums_ref, f32[2048,256]{1,0:T(8,128)S(1)} %get-tuple-element.24.rest_ref, ...), custom_call_target="tpu_custom_call" | custom-call | flops 1000 | bytes 1000 | tf_op jit(solution)/shard_map/early/pallas_call | solution.py:267
  44.9 0.0 collective-permute-done.9.b2
  44.9 5.1 %late.1 = bf16[64,2048]{1,0:T(8,128)(2,1)} custom-call(bf16[2048,2560]{1,0:T(8,128)(2,1)S(1)} %get-tuple-element.21.masked_ref, f32[2048,128]{1,0:T(8,128)S(1)} %get-tuple-element.22.scale_ref, f32[2048,256]{1,0:T(8,128)S(1)} %early.1.sums_ref, f32[2048,256]{1,0:T(8,128)S(1)} %get-tuple-element.24.rest_ref, ...), custom_call_target="tpu_custom_call" | custom-call | tf_op jit(solution)/shard_map/late/pallas_call | solution.py:278
Async XLA Ops:
  2.9 26.2 %all-to-all-start = ((bf16[64,8,256]{2,1,0:T(8,128)(2,1)}), bf16[64,8,256]{2,1,0:T(8,128)(2,1)S(1)}, u32[]{:S(2)}, u32[]{:S(2)}) async-start(bf16[64,8,256]{2,1,0:T(8,128)(2,1)} %bitcast.4), calls=%async_computation | async-start | bytes 524288 | tf_op jit(solution)/shard_map/all_to_all | solution.py:228
  15.9 6.3 %collective-permute-start = (bf16[352,256]{1,0:T(8,128)(2,1)S(1)}, bf16[352,256]{1,0:T(8,128)(2,1)S(1)}, u32[]{:S(2)}, u32[]{:S(2)}) collective-permute-start(bf16[352,256]{1,0:T(8,128)(2,1)S(1)} %get-tuple-element.19.a0), channel_id=1, source_target_pairs={{1,0},{2,1},{3,2},{0,3},{5,4},{6,5},{7,6},{4,7},{9,8},{10,9},{11,1... | collective-permute-start | bytes 540680 | tf_op jit(solution)/shard_map/ppermute | solution.py:190
  18.7 6.9 %collective-permute-start.4 = (bf16[352,256]{1,0:T(8,128)(2,1)S(1)}, bf16[352,256]{1,0:T(8,128)(2,1)S(1)}, u32[]{:S(2)}, u32[]{:S(2)}) collective-permute-start(bf16[352,256]{1,0:T(8,128)(2,1)S(1)} %get-tuple-element.20.b0), channel_id=1, source_target_pairs={{3,0},{0,1},{1,2},{2,3},{7,4},{4,5},{5,6},{6,7},{11,8},{8,9},{9,10... | collective-permute-start | bytes 540680 | tf_op jit(solution)/shard_map/ppermute | solution.py:190
  18.7 11.9 %collective-permute-start.2 = (bf16[352,256]{1,0:T(8,128)(2,1)S(1)}, bf16[352,256]{1,0:T(8,128)(2,1)S(1)}, u32[]{:S(2)}, u32[]{:S(2)}) collective-permute-start(bf16[352,256]{1,0:T(8,128)(2,1)S(1)} %get-tuple-element.19.a0), channel_id=1, source_target_pairs={{3,0},{0,1},{1,2},{2,3},{7,4},{4,5},{5,6},{6,7},{11,8},{8,9},{9,10... | collective-permute-start | bytes 540680 | tf_op jit(solution)/shard_map/ppermute | solution.py:190
  18.7 13.4 %collective-permute-start.3 = (bf16[352,256]{1,0:T(8,128)(2,1)S(1)}, bf16[352,256]{1,0:T(8,128)(2,1)S(1)}, u32[]{:S(2)}, u32[]{:S(2)}) collective-permute-start(bf16[352,256]{1,0:T(8,128)(2,1)S(1)} %get-tuple-element.20.b0), channel_id=1, source_target_pairs={{1,0},{2,1},{3,2},{0,3},{5,4},{6,5},{7,6},{4,7},{9,8},{10,9},{11,1... | collective-permute-start | bytes 540680 | tf_op jit(solution)/shard_map/ppermute | solution.py:190
  22.2 11.5 %collective-permute-start.1 = (bf16[352,256]{1,0:T(8,128)(2,1)S(1)}, bf16[352,256]{1,0:T(8,128)(2,1)S(1)}, u32[]{:S(2)}, u32[]{:S(2)}) collective-permute-start(bf16[352,256]{1,0:T(8,128)(2,1)S(1)} %collective-permute-done.a1), channel_id=1, source_target_pairs={{1,0},{2,1},{3,2},{0,3},{5,4},{6,5},{7,6},{4,7},{9,8},{10,9},{11,1... | collective-permute-start | bytes 540680 | tf_op jit(solution)/shard_map/ppermute | solution.py:190
  25.6 13.4 %collective-permute-start.5 = (bf16[352,256]{1,0:T(8,128)(2,1)S(1)}, bf16[352,256]{1,0:T(8,128)(2,1)S(1)}, u32[]{:S(2)}, u32[]{:S(2)}) collective-permute-start(bf16[352,256]{1,0:T(8,128)(2,1)S(1)} %collective-permute-done.4.b3), channel_id=1, source_target_pairs={{3,0},{0,1},{1,2},{2,3},{7,4},{4,5},{5,6},{6,7},{11,8},{8,9},{9,10... | collective-permute-start | bytes 540680 | tf_op jit(solution)/shard_map/ppermute | solution.py:190
  29.1 4.7 %copy-start = (bf16[2048,2560]{1,0:T(8,128)(2,1)S(1)}, bf16[2048,2560]{1,0:T(8,128)(2,1)}, u32[]{:S(2)}) copy-start(bf16[2048,2560]{1,0:T(8,128)(2,1)} %adj_ref.1) | copy-start | bytes 31457284
  29.1 4.7 %copy-start.1 = (s32[16,20]{1,0:T(8,128)S(1)}, s32[16,20]{1,0:T(8,128)}, u32[]{:S(2)}) copy-start(s32[16,20]{1,0:T(8,128)} %mask_ref.1) | copy-start | bytes 3844
  29.3 12.1 %collective-permute-start.8 = (bf16[768,128]{1,0:T(8,128)(2,1)S(1)}, bf16[768,128]{1,0:T(8,128)(2,1)S(1)}, u32[]{:S(2)}, u32[]{:S(2)}) collective-permute-start(bf16[768,128]{1,0:T(8,128)(2,1)S(1)} %get-tuple-element.26.b0), channel_id=1, source_target_pairs={{3,0},{0,1},{1,2},{2,3},{7,4},{4,5},{5,6},{6,7},{11,8},{8,9},{9,10... | collective-permute-start | bytes 589832 | tf_op jit(solution)/shard_map/ppermute | solution.py:190
  30.6 10.8 %collective-permute-start.6 = (bf16[768,128]{1,0:T(8,128)(2,1)S(1)}, bf16[768,128]{1,0:T(8,128)(2,1)S(1)}, u32[]{:S(2)}, u32[]{:S(2)}) collective-permute-start(bf16[768,128]{1,0:T(8,128)(2,1)S(1)} %get-tuple-element.26.b0), channel_id=1, source_target_pairs={{1,0},{2,1},{3,2},{0,3},{5,4},{6,5},{7,6},{4,7},{9,8},{10,9},{11,1... | collective-permute-start | bytes 589832 | tf_op jit(solution)/shard_map/ppermute | solution.py:190
  32.2 9.2 %collective-permute-start.7 = (bf16[256,128]{1,0:T(8,128)(2,1)S(1)}, bf16[256,128]{1,0:T(8,128)(2,1)S(1)}, u32[]{:S(2)}, u32[]{:S(2)}) collective-permute-start(bf16[256,128]{1,0:T(8,128)(2,1)S(1)} %get-tuple-element.27), channel_id=1, source_target_pairs={{2,0},{3,1},{0,2},{1,3},{6,4},{7,5},{4,6},{5,7},{10,8},{11,9},{8,1... | collective-permute-start | bytes 196616 | tf_op jit(solution)/shard_map/ppermute | solution.py:190
  36.5 8.4 %collective-permute-start.9 = (bf16[512,128]{1,0:T(8,128)(2,1)S(1)}, bf16[512,128]{1,0:T(8,128)(2,1)S(1)}, u32[]{:S(2)}, u32[]{:S(2)}) collective-permute-start(bf16[512,128]{1,0:T(8,128)(2,1)S(1)} %get-tuple-element.28), channel_id=1, source_target_pairs={{2,0},{3,1},{0,2},{1,3},{6,4},{7,5},{4,6},{5,7},{10,8},{11,9},{8,1... | collective-permute-start | bytes 393224 | tf_op jit(solution)/shard_map/ppermute | solution.py:190

commit v6 on v4

--- a/solution.py
+++ b/solution.py
@@ -79,7 +79,7 @@
 def prep_kernel(mask_ref, adj_ref, far_ref, _, __, ___, masked_ref, scale_ref, later_ref):
     later_ref[...] = far_ref[...]
     rows, cols = masked_ref.shape
-    step = 16
+    step = 32
     for i in range(rows // TILE):
         keep = [jnp.full((1, TILE), mask_ref[i, t].astype(F32), F32) for t in range(cols // TILE)]
         keep = jnp.concatenate(keep, axis=1).astype(BF)

time: 50.2 us -> 50.2 us (level)
  no operation moved by 1% of the time
where the time goes in v6:
time: 50.2 us; the launch traced here: 50 us
  starting transfers between devices  28.9 us (58%)
  Pallas kernels  16.8 us (33%)
  waiting for transfers between devices  4.24 us (8%)
    ppermute x10, starting transfers between devices, ring(): return lax.ppermute(x, 'feat', [((i + shift) % 4, i) for i in range(4)])  15.9 us
    all_to_all x1, starting transfers between devices, local(): lax.all_to_all(outgoing.reshape(peers, slots, full), 'dom', split_axis=0,...  13 us
    pallas_call x1, Pallas kernels, local(): pl.pallas_call(late_kernel, out_shape=jax.ShapeDtypeStruct((width, rows),...  5.15 us
    all_to_all x1, waiting for transfers between devices, local(): lax.all_to_all(outgoing.reshape(peers, slots, full), 'dom', split_axis=0,...  3.46 us
    pallas_call x1, Pallas kernels, local(): pl.pallas_call(early_kernel, out_shape=pltpu.VMEM((rows, full), F32), in_...  3.46 us
    pallas_call x1, Pallas kernels, local(): pl.pallas_call(pick_kernel, out_shape=[pltpu.VMEM((halo, full), BF)] + [p...  2.89 us
    pallas_call x1, Pallas kernels, local(): pl.pallas_call(prep_kernel, out_shape=[pltpu.VMEM((rows, cols), BF), pltp...  2.72 us
    pallas_call x1, Pallas kernels, local(): pl.pallas_call(own_kernel, out_shape=[pltpu.VMEM((rows, full), F32), pltp...  2.44 us
  transfers between devices with their start and end apart: 11, of which 2 were waited for; matrix products, arithmetic and copies ran while one was open for 0% of the time, Pallas kernels for 18%

profile of v6, /device:TPU:1, one launch (start us, length us, event | category | flops | bytes accessed | tf_op | source)
XLA Modules:
  0.0 50.0 jit_solution(5538105917380893959)
XLA Ops:
  0.0 2.9 %pick.1 = (bf16[512,256]{1,0:T(8,128)(2,1)}, bf16[352,256]{1,0:T(8,128)(2,1)S(1)}, bf16[352,256]{1,0:T(8,128)(2,1)S(1)}) custom-call(s32[8,64]{1,0:T(8,128)} %bitcast.12, bf16[64,2048]{1,0:T(8,128)(2,1)} %bitcast.11, bf16[2,64,2048]{2,1,0:T(8,128)(2,1)} %bitcast.10, bf16[3,64,256]{2,1,0:T(8,128)(2,1)} %weight_hbm.1), custom_call_target="tpu_custom_call" | custom-call | tf_op jit(solution)/shard_map/pick/pallas_call | solution.py:199
  2.9 13.0 %all-to-all-start = ((bf16[64,8,256]{2,1,0:T(8,128)(2,1)}), bf16[64,8,256]{2,1,0:T(8,128)(2,1)S(1)}, u32[]{:S(2)}, u32[]{:S(2)}) async-start(bf16[64,8,256]{2,1,0:T(8,128)(2,1)} %bitcast.4), calls=%async_computation | async-start | bytes 524288 | tf_op jit(solution)/shard_map/all_to_all | solution.py:218
  15.9 2.8 %collective-permute-start = (bf16[352,256]{1,0:T(8,128)(2,1)S(1)}, bf16[352,256]{1,0:T(8,128)(2,1)S(1)}, u32[]{:S(2)}, u32[]{:S(2)}) collective-permute-start(bf16[352,256]{1,0:T(8,128)(2,1)S(1)} %get-tuple-element.19.a0), channel_id=1, source_target_pairs={{1,0},{2,1},{3,2},{0,3},{5,4},{6,5},{7,6},{4,7},{9,8},{10,9},{11,1... | collective-permute-start | bytes 540680 | tf_op jit(solution)/shard_map/ppermute | solution.py:180
  18.7 0.0 collective-permute-start.4
  18.7 0.0 collective-permute-start.2
  18.7 2.7 %collective-permute-start.3 = (bf16[352,256]{1,0:T(8,128)(2,1)S(1)}, bf16[352,256]{1,0:T(8,128)(2,1)S(1)}, u32[]{:S(2)}, u32[]{:S(2)}) collective-permute-start(bf16[352,256]{1,0:T(8,128)(2,1)S(1)} %get-tuple-element.20.b0), channel_id=1, source_target_pairs={{1,0},{2,1},{3,2},{0,3},{5,4},{6,5},{7,6},{4,7},{9,8},{10,9},{11,1... | collective-permute-start | bytes 540680 | tf_op jit(solution)/shard_map/ppermute | solution.py:180
  21.4 0.8 %collective-permute-done.a1 = bf16[352,256]{1,0:T(8,128)(2,1)S(1)} collective-permute-done((bf16[352,256]{1,0:T(8,128)(2,1)S(1)}, bf16[352,256]{1,0:T(8,128)(2,1)S(1)}, u32[]{:S(2)}, u32[]{:S(2)}) %collective-permute-start) | collective-permute-done | bytes 180256 | tf_op jit(solution)/shard_map/ppermute | solution.py:180
  22.2 3.4 %collective-permute-start.1 = (bf16[352,256]{1,0:T(8,128)(2,1)S(1)}, bf16[352,256]{1,0:T(8,128)(2,1)S(1)}, u32[]{:S(2)}, u32[]{:S(2)}) collective-permute-start(bf16[352,256]{1,0:T(8,128)(2,1)S(1)} %collective-permute-done.a1), channel_id=1, source_target_pairs={{1,0},{2,1},{3,2},{0,3},{5,4},{6,5},{7,6},{4,7},{9,8},{10,9},{11,1... | collective-permute-start | bytes 540680 | tf_op jit(solution)/shard_map/ppermute | solution.py:180
  25.6 0.0 collective-permute-done.4.b3
  25.6 0.0 collective-permute-start.5
  25.6 3.5 %all-to-all-done = bf16[64,8,256]{2,1,0:T(8,128)(2,1)S(1)} async-done(((bf16[64,8,256]{2,1,0:T(8,128)(2,1)}), bf16[64,8,256]{2,1,0:T(8,128)(2,1)S(1)}, u32[]{:S(2)}, u32[]{:S(2)}) %all-to-all-start) | async-done | bytes 262176 | tf_op jit(solution)/shard_map/all_to_all | solution.py:218
  29.1 0.0 copy-start
  29.1 0.0 copy-start.1
  29.1 0.2 compact.1
  29.3 1.4 %collective-permute-start.8 = (bf16[768,128]{1,0:T(8,128)(2,1)S(1)}, bf16[768,128]{1,0:T(8,128)(2,1)S(1)}, u32[]{:S(2)}, u32[]{:S(2)}) collective-permute-start(bf16[768,128]{1,0:T(8,128)(2,1)S(1)} %get-tuple-element.26.b0), channel_id=1, source_target_pairs={{3,0},{0,1},{1,2},{2,3},{7,4},{4,5},{5,6},{6,7},{11,8},{8,9},{9,10... | collective-permute-start | bytes 589832 | tf_op jit(solution)/shard_map/ppermute | solution.py:180
  30.6 0.0 collective-permute-done.2.__.a3
  30.6 1.5 %collective-permute-start.6 = (bf16[768,128]{1,0:T(8,128)(2,1)S(1)}, bf16[768,128]{1,0:T(8,128)(2,1)S(1)}, u32[]{:S(2)}, u32[]{:S(2)}) collective-permute-start(bf16[768,128]{1,0:T(8,128)(2,1)S(1)} %get-tuple-element.26.b0), channel_id=1, source_target_pairs={{1,0},{2,1},{3,2},{0,3},{5,4},{6,5},{7,6},{4,7},{9,8},{10,9},{11,1... | collective-permute-start | bytes 589832 | tf_op jit(solution)/shard_map/ppermute | solution.py:180
  32.2 0.0 collective-permute-done.3.___.b1
  32.2 1.5 %collective-permute-start.7 = (bf16[256,128]{1,0:T(8,128)(2,1)S(1)}, bf16[256,128]{1,0:T(8,128)(2,1)S(1)}, u32[]{:S(2)}, u32[]{:S(2)}) collective-permute-start(bf16[256,128]{1,0:T(8,128)(2,1)S(1)} %get-tuple-element.27), channel_id=1, source_target_pairs={{2,0},{3,1},{0,2},{1,3},{6,4},{7,5},{4,6},{5,7},{10,8},{11,9},{8,1... | collective-permute-start | bytes 196616 | tf_op jit(solution)/shard_map/ppermute | solution.py:180
  33.7 0.0 collective-permute-done.1._.a2
  33.7 0.0 copy-done
  33.7 0.0 copy-done.1
  33.7 2.7 %prep.1 = (bf16[2048,2560]{1,0:T(8,128)(2,1)S(1)}, f32[2048,128]{1,0:T(8,128)S(1)}, bf16[512,128]{1,0:T(8,128)(2,1)S(1)}) custom-call(s32[16,20]{1,0:T(8,128)S(1)} %copy-done.1, bf16[2048,2560]{1,0:T(8,128)(2,1)S(1)} %copy-done, bf16[512,128]{1,0:T(8,128)(2,1)S(1)} %get-tuple-element.18.far_ref, bf16[352,256]{1,0:T(8,128)(2,1)S(1)} %collective-permute-done.1._.a2, ...), custom_call_target="tpu_custom_call" | custom-call | flops 4300000768 | bytes 1000 | tf_op jit(solution)/shard_map/prep/pallas_call | solution.py:231
  36.5 2.5 %collective-permute-start.9 = (bf16[512,128]{1,0:T(8,128)(2,1)S(1)}, bf16[512,128]{1,0:T(8,128)(2,1)S(1)}, u32[]{:S(2)}, u32[]{:S(2)}) collective-permute-start(bf16[512,128]{1,0:T(8,128)(2,1)S(1)} %get-tuple-element.28), channel_id=1, source_target_pairs={{2,0},{3,1},{0,2},{1,3},{6,4},{7,5},{4,6},{5,7},{10,8},{11,9},{8,1... | collective-permute-start | bytes 393224 | tf_op jit(solution)/shard_map/ppermute | solution.py:180
  38.9 0.0 collective-permute-done.5.b2
  38.9 2.4 %own.1 = (f32[2048,256]{1,0:T(8,128)S(1)}, f32[2048,256]{1,0:T(8,128)S(1)}, bf16[3,256,256]{2,1,0:T(8,128)(2,1)S(1)}) custom-call(s32[1]{0:T(128)} %bitcast.6.place_ref, bf16[2048,2560]{1,0:T(8,128)(2,1)S(1)} %get-tuple-element.21.masked_ref, bf16[352,256]{1,0:T(8,128)(2,1)S(1)} %get-tuple-element.19.a0, bf16[352,256]{1,0:T(8,128)(2,1)S(1)} %collective-permute-done.a1, ...), custom_call_target="tpu_custom_call" | custom-call | flops 2100001024 | bytes 1000 | tf_op jit(solution)/shard_map/own/pallas_call | solution.py:242
  41.4 0.0 collective-permute-done.7.b2
  41.4 0.0 collective-permute-done.8.b3
  41.4 0.0 collective-permute-done.6.b1
  41.4 3.5 %early.1.sums_ref = f32[2048,256]{1,0:T(8,128)S(1)} custom-call(bf16[2048,2560]{1,0:T(8,128)(2,1)S(1)} %get-tuple-element.21.masked_ref, f32[2048,128]{1,0:T(8,128)S(1)} %get-tuple-element.22.scale_ref, f32[2048,256]{1,0:T(8,128)S(1)} %get-tuple-element.23.sums_ref, f32[2048,256]{1,0:T(8,128)S(1)} %get-tuple-element.24.rest_ref, ...), custom_call_target="tpu_custom_call" | custom-call | flops 1000 | bytes 1000 | tf_op jit(solution)/shard_map/early/pallas_call | solution.py:257
  44.9 0.0 collective-permute-done.9.b2
  44.9 5.1 %late.1 = bf16[64,2048]{1,0:T(8,128)(2,1)} custom-call(bf16[2048,2560]{1,0:T(8,128)(2,1)S(1)} %get-tuple-element.21.masked_ref, f32[2048,128]{1,0:T(8,128)S(1)} %get-tuple-element.22.scale_ref, f32[2048,256]{1,0:T(8,128)S(1)} %early.1.sums_ref, f32[2048,256]{1,0:T(8,128)S(1)} %get-tuple-element.24.rest_ref, ...), custom_call_target="tpu_custom_call" | custom-call | tf_op jit(solution)/shard_map/late/pallas_call | solution.py:268
Async XLA Ops:
  2.9 26.2 %all-to-all-start = ((bf16[64,8,256]{2,1,0:T(8,128)(2,1)}), bf16[64,8,256]{2,1,0:T(8,128)(2,1)S(1)}, u32[]{:S(2)}, u32[]{:S(2)}) async-start(bf16[64,8,256]{2,1,0:T(8,128)(2,1)} %bitcast.4), calls=%async_computation | async-start | bytes 524288 | tf_op jit(solution)/shard_map/all_to_all | solution.py:218
  15.9 6.3 %collective-permute-start = (bf16[352,256]{1,0:T(8,128)(2,1)S(1)}, bf16[352,256]{1,0:T(8,128)(2,1)S(1)}, u32[]{:S(2)}, u32[]{:S(2)}) collective-permute-start(bf16[352,256]{1,0:T(8,128)(2,1)S(1)} %get-tuple-element.19.a0), channel_id=1, source_target_pairs={{1,0},{2,1},{3,2},{0,3},{5,4},{6,5},{7,6},{4,7},{9,8},{10,9},{11,1... | collective-permute-start | bytes 540680 | tf_op jit(solution)/shard_map/ppermute | solution.py:180
  18.7 6.9 %collective-permute-start.4 = (bf16[352,256]{1,0:T(8,128)(2,1)S(1)}, bf16[352,256]{1,0:T(8,128)(2,1)S(1)}, u32[]{:S(2)}, u32[]{:S(2)}) collective-permute-start(bf16[352,256]{1,0:T(8,128)(2,1)S(1)} %get-tuple-element.20.b0), channel_id=1, source_target_pairs={{3,0},{0,1},{1,2},{2,3},{7,4},{4,5},{5,6},{6,7},{11,8},{8,9},{9,10... | collective-permute-start | bytes 540680 | tf_op jit(solution)/shard_map/ppermute | solution.py:180
  18.7 11.9 %collective-permute-start.2 = (bf16[352,256]{1,0:T(8,128)(2,1)S(1)}, bf16[352,256]{1,0:T(8,128)(2,1)S(1)}, u32[]{:S(2)}, u32[]{:S(2)}) collective-permute-start(bf16[352,256]{1,0:T(8,128)(2,1)S(1)} %get-tuple-element.19.a0), channel_id=1, source_target_pairs={{3,0},{0,1},{1,2},{2,3},{7,4},{4,5},{5,6},{6,7},{11,8},{8,9},{9,10... | collective-permute-start | bytes 540680 | tf_op jit(solution)/shard_map/ppermute | solution.py:180
  18.7 13.4 %collective-permute-start.3 = (bf16[352,256]{1,0:T(8,128)(2,1)S(1)}, bf16[352,256]{1,0:T(8,128)(2,1)S(1)}, u32[]{:S(2)}, u32[]{:S(2)}) collective-permute-start(bf16[352,256]{1,0:T(8,128)(2,1)S(1)} %get-tuple-element.20.b0), channel_id=1, source_target_pairs={{1,0},{2,1},{3,2},{0,3},{5,4},{6,5},{7,6},{4,7},{9,8},{10,9},{11,1... | collective-permute-start | bytes 540680 | tf_op jit(solution)/shard_map/ppermute | solution.py:180
  22.2 11.5 %collective-permute-start.1 = (bf16[352,256]{1,0:T(8,128)(2,1)S(1)}, bf16[352,256]{1,0:T(8,128)(2,1)S(1)}, u32[]{:S(2)}, u32[]{:S(2)}) collective-permute-start(bf16[352,256]{1,0:T(8,128)(2,1)S(1)} %collective-permute-done.a1), channel_id=1, source_target_pairs={{1,0},{2,1},{3,2},{0,3},{5,4},{6,5},{7,6},{4,7},{9,8},{10,9},{11,1... | collective-permute-start | bytes 540680 | tf_op jit(solution)/shard_map/ppermute | solution.py:180
  25.6 13.4 %collective-permute-start.5 = (bf16[352,256]{1,0:T(8,128)(2,1)S(1)}, bf16[352,256]{1,0:T(8,128)(2,1)S(1)}, u32[]{:S(2)}, u32[]{:S(2)}) collective-permute-start(bf16[352,256]{1,0:T(8,128)(2,1)S(1)} %collective-permute-done.4.b3), channel_id=1, source_target_pairs={{3,0},{0,1},{1,2},{2,3},{7,4},{4,5},{5,6},{6,7},{11,8},{8,9},{9,10... | collective-permute-start | bytes 540680 | tf_op jit(solution)/shard_map/ppermute | solution.py:180
  29.1 4.7 %copy-start = (bf16[2048,2560]{1,0:T(8,128)(2,1)S(1)}, bf16[2048,2560]{1,0:T(8,128)(2,1)}, u32[]{:S(2)}) copy-start(bf16[2048,2560]{1,0:T(8,128)(2,1)} %adj_ref.1) | copy-start | bytes 31457284
  29.1 4.7 %copy-start.1 = (s32[16,20]{1,0:T(8,128)S(1)}, s32[16,20]{1,0:T(8,128)}, u32[]{:S(2)}) copy-start(s32[16,20]{1,0:T(8,128)} %mask_ref.1) | copy-start | bytes 3844
  29.3 12.1 %collective-permute-start.8 = (bf16[768,128]{1,0:T(8,128)(2,1)S(1)}, bf16[768,128]{1,0:T(8,128)(2,1)S(1)}, u32[]{:S(2)}, u32[]{:S(2)}) collective-permute-start(bf16[768,128]{1,0:T(8,128)(2,1)S(1)} %get-tuple-element.26.b0), channel_id=1, source_target_pairs={{3,0},{0,1},{1,2},{2,3},{7,4},{4,5},{5,6},{6,7},{11,8},{8,9},{9,10... | collective-permute-start | bytes 589832 | tf_op jit(solution)/shard_map/ppermute | solution.py:180
  30.6 10.8 %collective-permute-start.6 = (bf16[768,128]{1,0:T(8,128)(2,1)S(1)}, bf16[768,128]{1,0:T(8,128)(2,1)S(1)}, u32[]{:S(2)}, u32[]{:S(2)}) collective-permute-start(bf16[768,128]{1,0:T(8,128)(2,1)S(1)} %get-tuple-element.26.b0), channel_id=1, source_target_pairs={{1,0},{2,1},{3,2},{0,3},{5,4},{6,5},{7,6},{4,7},{9,8},{10,9},{11,1... | collective-permute-start | bytes 589832 | tf_op jit(solution)/shard_map/ppermute | solution.py:180
  32.2 9.2 %collective-permute-start.7 = (bf16[256,128]{1,0:T(8,128)(2,1)S(1)}, bf16[256,128]{1,0:T(8,128)(2,1)S(1)}, u32[]{:S(2)}, u32[]{:S(2)}) collective-permute-start(bf16[256,128]{1,0:T(8,128)(2,1)S(1)} %get-tuple-element.27), channel_id=1, source_target_pairs={{2,0},{3,1},{0,2},{1,3},{6,4},{7,5},{4,6},{5,7},{10,8},{11,9},{8,1... | collective-permute-start | bytes 196616 | tf_op jit(solution)/shard_map/ppermute | solution.py:180
  36.5 8.4 %collective-permute-start.9 = (bf16[512,128]{1,0:T(8,128)(2,1)S(1)}, bf16[512,128]{1,0:T(8,128)(2,1)S(1)}, u32[]{:S(2)}, u32[]{:S(2)}) collective-permute-start(bf16[512,128]{1,0:T(8,128)(2,1)S(1)} %get-tuple-element.28), channel_id=1, source_target_pairs={{2,0},{3,1},{0,2},{1,3},{6,4},{7,5},{4,6},{5,7},{10,8},{11,9},{8,1... | collective-permute-start | bytes 393224 | tf_op jit(solution)/shard_map/ppermute | solution.py:180
